TPU v7x, 256 devices: a whole 4x4x8 slice. The times are simulated.
256 devices in a mesh: ctx: 64 (over y, x_lo, z), tp: 4 (over x_hi, core).
Axes of the slice: x: 4 (x_hi: 2, x_lo: 2; x = x_hi * 2 + x_lo), y: 4, z: 8, core: 2. Of those that a mesh axis runs over, the one named last changes fastest.
Arguments:
- queries: bfloat16 [16384, 4096], P('ctx', 'tp'), may hold values from -8 to 8
- latent_keys: bfloat16 [512, 4096], P(('ctx', 'tp')), may hold values from -8 to 8
- latent_values: bfloat16 [512, 4096], P(('ctx', 'tp')), may hold values from -6 to 6
- gate_logit: float32 [], replicated, may hold values from 0.3 to 1.2
- last_frame: int32 [128], P('ctx'), may hold values from 0 to 7, as said below
- cotangent: bfloat16 [16384, 4096], P('ctx', 'tp'), may hold values from -6 to 6
Outputs:
- attended: bfloat16 [16384, 4096], P('ctx', 'tp')
- query_grad: bfloat16 [16384, 4096], P('ctx', 'tp')
- key_grad: float32 [512, 4096], P(('ctx', 'tp'))
- value_grad: float32 [512, 4096], P(('ctx', 'tp'))
Inputs may be any that keep to these rules, and one draw needn't show every extreme that they name: Non-decreasing along the document; text block b sees the frames 0 to last_frame[b].
All inputs are finite; a program needn't handle non-finite values.
Results may differ from a plain program's by a relative error of at most 0.015.
Values may be sent and summed in bfloat16 or wider, within the bound.
No kernel may reach another device: no remote copies, remote signals or barrier semaphores. Data moves between devices by JAX's collectives and lax.ppermute only.
A program may use at most 64 MiB of HBM per device.

v0:
```python
import jax
import jax.numpy as jnp
from jax import lax
from jax.sharding import PartitionSpec as P

DH = 128
LATF = 64
TBLK = 128


masked_fill = -1e30


def per_device(queries, latent_keys, latent_values, gate_logit, last_frame, cotangent):
    tok_rows, columns = queries.shape
    head_count = columns // DH
    keys_every, values_every = (
        lax.all_gather(latent_keys, ("ctx", "tp"), axis=0, tiled=True),
        lax.all_gather(latent_values, ("ctx", "tp"), axis=0, tiled=True),
    )
    offset = lax.axis_index("tp") * columns
    keys_mine = lax.dynamic_slice_in_dim(keys_every, offset, columns, 1)
    values_mine = lax.dynamic_slice_in_dim(values_every, offset, columns, 1)
    latent_count = keys_mine.shape[0]
    keys_heads = keys_mine.reshape(latent_count, head_count, DH)
    values_heads = values_mine.reshape(latent_count, head_count, DH)
    score_scale = 1.0 / DH**0.5
    gate_value = jnp.tanh(gate_logit)
    frame_index = jnp.arange(latent_count, dtype=jnp.int32) // LATF
    last_tok = jnp.repeat(last_frame, TBLK, total_repeat_length=tok_rows)
    block_rows = min(512, tok_rows)
    block_count = tok_rows // block_rows

    def advance(running, block_index):
        row_start = block_index * block_rows
        query_block = queries.reshape(block_rows, head_count, DH)
        last_block = lax.dynamic_slice_in_dim(last_tok, row_start, block_rows, 0)
        visible = frame_index[None, :] <= last_block[:, None]
        scores = (
            jnp.einsum("qhd,khd->hqk", query_block, keys_heads, preferred_element_type=jnp.float32)
            * score_scale
        )
        scores = jnp.where(visible[None], scores, masked_fill)
        maxima = jnp.max(scores, axis=-1, keepdims=True)
        expo = jnp.where(visible[None], jnp.exp(scores - maxima), 0.0)
        totals = jnp.sum(expo, axis=-1, keepdims=True)
        weights = expo / totals
        weights_low = weights.astype(jnp.bfloat16)
        context = jnp.einsum(
            "hqk,khd->qhd", weights_low, values_heads, preferred_element_type=jnp.float32
        )
        attended = (gate_value * context.reshape(block_rows, columns)).astype(jnp.bfloat16)
        gated_cot = (gate_value * cotangent.astype(jnp.float32)).astype(jnp.bfloat16)
        gated_heads = gated_cot.reshape(block_rows, head_count, DH)
        prob_grad = jnp.einsum(
            "qhd,khd->hqk", gated_heads, values_heads, preferred_element_type=jnp.float32
        )
        inner_sum = jnp.sum(weights * prob_grad, axis=-1, keepdims=True)
        score_grad = (weights * (prob_grad - inner_sum) * score_scale).astype(jnp.bfloat16)
        query_grad = jnp.einsum(
            "hqk,khd->qhd", score_grad, keys_heads, preferred_element_type=jnp.float32
        )
        key_part = jnp.einsum(
            "hqk,qhd->khd", score_grad, query_block, preferred_element_type=jnp.float32
        )
        value_part = jnp.einsum(
            "hqk,qhd->khd", weights_low, gated_heads, preferred_element_type=jnp.float32
        )
        query_low = query_grad.reshape(block_rows, columns).astype(jnp.bfloat16)
        return ((running[0] + key_part, running[1] + value_part), (attended, query_low))

    zeros_kv = jnp.zeros((latent_count, head_count, DH), jnp.float32)
    sums, outputs = lax.scan(
        advance, (zeros_kv, zeros_kv), jnp.arange(block_count, dtype=jnp.int32)
    )
    attended = outputs[0].reshape(tok_rows, columns)
    query_grad = outputs[1].reshape(tok_rows, columns)
    key_terms = sums[0].reshape(latent_count, columns)
    value_terms = sums[1].reshape(latent_count, columns)
    key_total, value_total = lax.psum((key_terms, value_terms), "ctx")
    portion = latent_count // lax.axis_size("ctx")
    first_row = lax.axis_index("ctx") * portion
    key_own = lax.dynamic_slice_in_dim(key_total, first_row, portion, 0)
    value_own = lax.dynamic_slice_in_dim(value_total, first_row, portion, 0)
    key_grad, value_grad = (
        lax.all_to_all(
            key_own.astype(jnp.bfloat16), "tp", split_axis=0, concat_axis=1, tiled=True
        ).astype(key_own.dtype),
        lax.all_to_all(
            value_own.astype(jnp.bfloat16), "tp", split_axis=0, concat_axis=1, tiled=True
        ).astype(value_own.dtype),
    )
    return (attended, query_grad, key_grad, value_grad)


def solution(mesh):
    placed = (
        P("ctx", "tp"),
        P(("ctx", "tp"), None),
        P(("ctx", "tp"), None),
        P(),
        P("ctx"),
        P("ctx", "tp"),
    )
    return jax.shard_map(
        per_device,
        mesh=mesh,
        in_specs=placed,
        out_specs=(P("ctx", "tp"), P("ctx", "tp"), P(("ctx", "tp"), None), P(("ctx", "tp"), None)),
        check_vma=False,
    )
```

profile of v0, /device:TPU:1, one launch (start us, length us, event | category | flops | bytes accessed | tf_op | source)
XLA Modules:
  0.0 1265.6 jit_solution(15816836092543142598)
XLA Ops:
  7.2 0.0 all-gather.7.cloned.1.call-start
  7.2 0.7 all-gather.7.cloned.1.call-update
  7.9 0.0 all-gather.5.cloned.1.call-start
  7.9 0.7 all-gather.5.cloned.1.call-update
  9.3 2.0 copy.89
  11.4 1.1 multiply_convert_fusion.1
  12.5 1.0 copy.90
  13.5 1.3 fusion.37
  14.9 1.3 compare_select_fusion.1
  16.2 0.1 broadcast_compare_fusion
  16.3 410.5 %all-gather.7.cloned.1.call-done = bf16[256,2,4096]{2,1,0:T(2,128)(2,1)} async-done(((bf16[1,2,4096]{2,1,0:T(2,128)(2,1)}), bf16[256,2,4096]{2,1,0:T(2,128)(2,1)}) %all-gather.7.cloned.1.call-update) | async-done | bytes 4194320 | tf_op jit(solution)/shard_map/all_gather | solution.py:18
  426.8 7.2 reshape.212
  434.0 406.2 %all-gather.5.cloned.1.call-done = bf16[256,2,4096]{2,1,0:T(2,128)(2,1)} async-done(((bf16[1,2,4096]{2,1,0:T(2,128)(2,1)}), bf16[256,2,4096]{2,1,0:T(2,128)(2,1)}) %all-gather.5.cloned.1.call-update) | async-done | bytes 4194320 | tf_op jit(solution)/shard_map/all_gather | solution.py:19
  840.2 7.2 reshape.210
  847.4 1.7 constant_dynamic-slice_fusion
  849.2 0.5 copy.88
  849.7 0.5 copy.64
  850.3 0.0 copy-start.1
  850.3 0.0 copy-start.3
  850.3 4.2 fusion.39
  854.5 0.0 copy-done.3
  854.5 3.8 fusion.38
  858.3 0.0 copy-done.1
  858.3 0.0 copy-start
  858.3 3.6 fusion.17
  861.9 0.0 copy-done
  861.9 0.0 copy-done.5
  861.9 2.2 fusion.21
  864.1 8.6 fusion.7
  872.7 1.9 copy.75
  874.6 0.0 copy-start.2
  874.6 3.0 copy.78
  877.6 302.5 %all-reduce.2 = (bf16[512,1024]{1,0:T(8,128)(2,1)}, bf16[512,1024]{1,0:T(8,128)(2,1)}) all-reduce(f32[512,1024]{1,0:T(8,128)S(1)} %copy.75, f32[512,1024]{1,0:T(8,128)} %copy.78), channel_id=1, replica_groups=mesh['ctx'=64,'tp'=4] {'ctx'}, use_global_device_ids=true, to_apply=%region_3.4 | all-reduce | flops 1048576 | bytes 6291456 | tf_op jit(solution)/shard_map/psum | solution.py:80
  1180.1 0.7 dynamic-slice_convert_fusion.1
  1180.8 0.6 all_to_all.20
  1181.4 58.1 %all-to-all-start = ((bf16[4,2,1024]{2,1,0:T(2,128)(2,1)}), bf16[4,2,1024]{2,1,0:T(2,128)(2,1)S(1)}, u32[]{:S(2)}, u32[]{:S(2)}) async-start(bf16[4,2,1024]{2,1,0:T(2,128)(2,1)} %all_to_all.20), calls=%async_computation | async-start | bytes 32768 | tf_op jit(solution)/shard_map/all_to_all | solution.py:86
  1239.5 0.7 dynamic-slice_convert_fusion
  1240.2 0.6 all_to_all.22
  1240.9 3.3 all-to-all-done
  1244.2 4.0 all-to-all-start.1
  1248.1 0.0 copy-done.2
  1248.1 7.4 fusion.18
  1255.5 0.0 copy-done.4
  1255.5 1.0 copy.79
  1256.5 1.0 copy.80
  1257.5 0.6 convert_element_type.82
  1258.1 0.0 all-to-all-done.1
  1258.1 0.6 convert_element_type.83
  (6 shorter events, 0.0 us)
Async XLA Ops:
  7.2 419.6 %all-gather.7.cloned.1.call-start = ((), (), s32[]{:S(2)}) async-start(), calls=%async_computation.3 | async-start | bytes 4210688 | tf_op jit(solution)/shard_map/all_gather | solution.py:18
  7.9 832.3 %all-gather.5.cloned.1.call-start = ((), (), s32[]{:S(2)}) async-start(), calls=%async_computation.2 | async-start | bytes 4210688 | tf_op jit(solution)/shard_map/all_gather | solution.py:19
  850.3 8.0 copy-start.1
  850.3 4.2 copy-start.3
  858.3 3.6 copy-start
  858.3 3.6 copy-start.5
  874.6 373.5 %copy-start.2 = (bf16[512,1024]{0,1:T(8,128)(2,1)S(1)}, bf16[512,1024]{0,1:T(8,128)(2,1)}, u32[]{:S(2)}) copy-start(bf16[512,1024]{0,1:T(8,128)(2,1)} %copy-done.1) | copy-start | bytes 3145732
  1181.4 62.8 %all-to-all-start = ((bf16[4,2,1024]{2,1,0:T(2,128)(2,1)}), bf16[4,2,1024]{2,1,0:T(2,128)(2,1)S(1)}, u32[]{:S(2)}, u32[]{:S(2)}) async-start(bf16[4,2,1024]{2,1,0:T(2,128)(2,1)} %all_to_all.20), calls=%async_computation | async-start | bytes 32768 | tf_op jit(solution)/shard_map/all_to_all | solution.py:86
  1244.2 14.0 %all-to-all-start.1 = ((bf16[4,2,1024]{2,1,0:T(2,128)(2,1)}), bf16[4,2,1024]{2,1,0:T(2,128)(2,1)S(1)}, u32[]{:S(2)}, u32[]{:S(2)}) async-start(bf16[4,2,1024]{2,1,0:T(2,128)(2,1)} %all_to_all.22), calls=%async_computation.1 | async-start | bytes 32768 | tf_op jit(solution)/shard_map/all_to_all | solution.py:89
  1248.1 7.4 copy-start.4
Sparse Core Ops, SparseCore 0:
  9.9 416.8 all-gather.6
  428.7 411.5 all-gather.4
where the time goes:
time: 1270 us
  waiting for transfers between devices  821 us (65%)
  blocking collectives  302 us (24%)
  starting transfers between devices  62.1 us (5%)
  local copies, waits for them, and re-layouts  31.2 us (2%)
  matrix products  29.7 us (2%)
  between operations  14.8 us (1%)
    all_gather x1, waiting for transfers between devices, per_device(): lax.all_gather(latent_keys, ('ctx', 'tp'), axis=0, tiled=True)  410 us
    all_gather x1, waiting for transfers between devices, per_device(): lax.all_gather(latent_values, ('ctx', 'tp'), axis=0, tiled=True)  406 us
    psum x1, blocking collectives, per_device(): key_total, value_total = lax.psum((key_terms, value_terms), 'ctx')  302 us
    all_to_all x1, starting transfers between devices, per_device(): lax.all_to_all(key_own.astype(jnp.bfloat16), 'tp', split_axis=0, concat_a...  58.1 us
  transfers between devices with their start and end apart: 4, of which 3 were waited for; matrix products, arithmetic and copies ran while one was open for 2% of the time, Pallas kernels for 0%

commit v1 on v0

v1 whole, which is shorter than its diff:
```python
import functools
import math

import jax
import jax.numpy as jnp
from jax import lax
from jax.experimental import pallas as pl
from jax.experimental.pallas import tpu as pltpu
from jax.sharding import PartitionSpec as P

DH = 128
LATF = 64
TBLK = 128
GROUP = 8
ZSIZE = 8
TP = 4
EXTRA = 16

masked_fill = -1e30
SCALE = 1.0 / DH**0.5
LOG2E = math.log2(math.e)
PARAMS = pltpu.CompilerParams(vmem_limit_bytes=32 * 2**20)
SMEM = pl.BlockSpec(memory_space=pltpu.SMEM)
VMEM = pl.BlockSpec(memory_space=pltpu.VMEM)


def pack_kernel(place_ref, last_ref, q_ref, c_ref, *out_refs):
    tok = q_ref.shape[0]
    group = place_ref[0]
    half = EXTRA // 2
    rows = lax.broadcasted_iota(jnp.int32, (EXTRA, DH), 0)
    frames = jnp.where(rows < half, last_ref[0], last_ref[1])
    frames = frames.astype(jnp.float32).astype(jnp.bfloat16)
    for k, out in enumerate(out_refs):
        cols = pl.ds(pl.multiple_of((group ^ k) * DH, DH), DH)
        out[0:tok, :] = q_ref[:, cols]
        out[tok : 2 * tok, :] = c_ref[:, cols]
        out[2 * tok : 2 * tok + EXTRA, :] = frames


def unpack_kernel(place_ref, *refs):
    block_refs, (att_ref, dq_ref) = refs[:GROUP], refs[GROUP:]
    tok = att_ref.shape[0]
    group = place_ref[0]
    for k, block in enumerate(block_refs):
        cols = pl.ds(pl.multiple_of((group ^ k) * DH, DH), DH)
        att_ref[:, cols] = block[0:tok, :]
        dq_ref[:, cols] = block[tok : 2 * tok, :]


def dot(a, b, dims):
    return lax.dot_general(a, b, (dims, ((), ())), preferred_element_type=jnp.float32)


def attention_kernel(gate_ref, k_ref, v_ref, *refs):
    msgs, outs = refs[:GROUP], refs[GROUP : 2 * GROUP]
    dk_ref, dv_ref, in_s, out_s, dk_s, dv_s = refs[2 * GROUP :]
    tok = outs[0].shape[0] // 2
    lat = k_ref.shape[0]
    gate = gate_ref[0]
    for j, msg in enumerate(msgs):
        in_s[j] = msg[...]
    dk_s[...] = jnp.zeros_like(dk_s)
    dv_s[...] = jnp.zeros_like(dv_s)
    frame = (lax.broadcasted_iota(jnp.int32, (1, lat), 1) // LATF).astype(jnp.float32)

    def step(j, carry):
        keys, values = k_ref[...], v_ref[...]
        q = in_s[j, 0:tok, :]
        cot = in_s[j, tok : 2 * tok, :]
        gcot = (gate * cot.astype(jnp.float32)).astype(jnp.bfloat16)
        scores = dot(q, keys, ((1,), (1,))) * (SCALE * LOG2E)
        parts = []
        for i in range(tok // TBLK):
            row = 2 * tok + i * (EXTRA // 2)
            last = in_s[j, row : row + 1, :].astype(jnp.float32)
            last = jnp.concatenate([last] * (lat // DH), axis=1)
            bias = jnp.where(frame <= last, 0.0, masked_fill)
            parts.append(scores[i * TBLK : (i + 1) * TBLK] + bias)
        scores = jnp.concatenate(parts, axis=0)
        expo = jnp.exp2(scores - jnp.max(scores, axis=-1, keepdims=True))
        weights = expo * (1.0 / jnp.sum(expo, axis=-1, keepdims=True))
        low = weights.astype(jnp.bfloat16)
        context = dot(low, values, ((1,), (0,)))
        out_s[j, 0:tok, :] = (gate * context).astype(jnp.bfloat16)
        prob_grad = dot(gcot, values, ((1,), (1,)))
        inner = jnp.sum(weights * prob_grad, axis=-1, keepdims=True)
        sgrad = (weights * (prob_grad - inner) * SCALE).astype(jnp.bfloat16)
        out_s[j, tok : 2 * tok, :] = dot(sgrad, keys, ((1,), (0,))).astype(jnp.bfloat16)
        dk_s[...] += dot(sgrad, q, ((0,), (0,)))
        dv_s[...] += dot(low, gcot, ((0,), (0,)))
        return carry

    lax.fori_loop(0, GROUP, step, 0)
    for j, out in enumerate(outs):
        out[...] = out_s[j]
    dk_ref[...] = dk_s[...].astype(jnp.bfloat16)
    dv_ref[...] = dv_s[...].astype(jnp.bfloat16)


def per_device(queries, latent_keys, latent_values, gate_logit, last_frame, cotangent):
    tok, columns = queries.shape
    own, wide = latent_keys.shape
    everyone = ("ctx", "tp")
    devices = GROUP * ZSIZE * TP
    lat = own * devices
    group = lax.axis_index("ctx") // ZSIZE
    place = group.astype(jnp.int32).reshape(1)
    gate = jnp.tanh(gate_logit).astype(jnp.float32).reshape(1)

    both = jnp.stack([latent_keys, latent_values]).reshape(2 * own, TP, GROUP, DH)
    both = both.transpose(2, 1, 0, 3)[:, None]
    both = jnp.broadcast_to(both, (GROUP, ZSIZE, TP, 2 * own, DH)).reshape(devices, 2 * own, DH)
    both = lax.all_to_all(both, everyone, 0, 0)
    keys = both[:, :own].reshape(lat, DH)
    values = both[:, own:].reshape(lat, DH)

    def swap(x, k):
        pairs = [(i, i ^ (k * ZSIZE)) for i in range(GROUP * ZSIZE)]
        return x if k == 0 else lax.ppermute(x, "ctx", pairs)

    msg_shape = jax.ShapeDtypeStruct((2 * tok + EXTRA, DH), jnp.bfloat16)
    back_shape = jax.ShapeDtypeStruct((2 * tok, DH), jnp.bfloat16)
    msgs = pl.pallas_call(
        pack_kernel,
        out_shape=[msg_shape] * GROUP,
        in_specs=[SMEM, SMEM, VMEM, VMEM],
        out_specs=[VMEM] * GROUP,
        compiler_params=PARAMS,
        name="pack",
    )(place, last_frame, queries, cotangent)
    msgs = [swap(m, k) for k, m in enumerate(msgs)]

    grad_shape = jax.ShapeDtypeStruct((lat, DH), jnp.bfloat16)
    *backs, key_terms, value_terms = pl.pallas_call(
        attention_kernel,
        out_shape=[back_shape] * GROUP + [grad_shape] * 2,
        in_specs=[SMEM] + [VMEM] * (2 + GROUP),
        out_specs=[VMEM] * (GROUP + 2),
        scratch_shapes=[
            pltpu.VMEM((GROUP, 2 * tok + EXTRA, DH), jnp.bfloat16),
            pltpu.VMEM((GROUP, 2 * tok, DH), jnp.bfloat16),
            pltpu.VMEM((lat, DH), jnp.float32),
            pltpu.VMEM((lat, DH), jnp.float32),
        ],
        compiler_params=PARAMS,
        name="attention",
    )(gate, keys, values, *msgs)

    terms = jnp.concatenate(
        [key_terms.reshape(devices, own, DH), value_terms.reshape(devices, own, DH)], axis=1
    )
    terms = lax.all_to_all(terms, everyone, 0, 0)
    backs = [swap(b, k) for k, b in enumerate(backs)]
    out_shape = jax.ShapeDtypeStruct((tok, columns), jnp.bfloat16)
    attended, query_grad = pl.pallas_call(
        unpack_kernel,
        out_shape=[out_shape] * 2,
        in_specs=[SMEM] + [VMEM] * GROUP,
        out_specs=[VMEM] * 2,
        compiler_params=PARAMS,
        name="unpack",
    )(place, *backs)
    sums = jnp.sum(
        terms.astype(jnp.float32).reshape(GROUP, ZSIZE, TP, 2 * own, DH), axis=1
    )
    sums = sums.transpose(2, 1, 0, 3).reshape(2, own, wide)
    return (attended, query_grad, sums[0], sums[1])


def solution(mesh):
    placed = (
        P("ctx", "tp"),
        P(("ctx", "tp"), None),
        P(("ctx", "tp"), None),
        P(),
        P("ctx"),
        P("ctx", "tp"),
    )
    return jax.shard_map(
        per_device,
        mesh=mesh,
        in_specs=placed,
        out_specs=(P("ctx", "tp"), P("ctx", "tp"), P(("ctx", "tp"), None), P(("ctx", "tp"), None)),
        check_vma=False,
    )
```

time: 1270 us -> 88.7 us (0.07)
  the two profiles are of different devices: /device:TPU:1 before, /device:TPU:2 now
where the time goes in v1:
time: 88.7 us; the launch traced here: 88.5 us
  starting transfers between devices  53.3 us (60%)
  waiting for transfers between devices  17.7 us (20%)
  Pallas kernels  11 us (12%)
  local copies, waits for them, and re-layouts  2.98 us (3%)
  other arithmetic  1.97 us (2%)
  between operations  1.47 us (2%)
    ppermute x14, starting transfers between devices, swap(): return x if k == 0 else lax.ppermute(x, 'ctx', pairs)  26.6 us
    ppermute x14, waiting for transfers between devices, swap(): return x if k == 0 else lax.ppermute(x, 'ctx', pairs)  17.7 us
    all_to_all x1, starting transfers between devices, per_device(): both = lax.all_to_all(both, everyone, 0, 0)  14.7 us
    all_to_all x1, starting transfers between devices, per_device(): terms = lax.all_to_all(terms, everyone, 0, 0)  12 us
    pallas_call x1, Pallas kernels, per_device(): pl.pallas_call(attention_kernel, out_shape=[back_shape] * GROUP + [grad_s...  8.91 us
    unnamed x9, local copies, waits for them, and re-layouts  1.94 us
  transfers between devices with their start and end apart: 16, of which 7 were waited for; matrix products, arithmetic and copies ran while one was open for 0% of the time, Pallas kernels for 2%

profile of v1, /device:TPU:2, one launch (start us, length us, event | category | flops | bytes accessed | tf_op | source)
XLA Modules:
  0.0 88.5 jit_solution(13703462902237098211)
XLA Ops:
  0.6 0.0 copy-start
  0.6 0.0 copy-start.1
  0.7 0.9 pad_maximum_fusion.1
  1.6 0.8 broadcast_in_dim.2
  2.4 14.7 %all-to-all-start = ((bf16[256,4,128]{2,1,0:T(4,128)(2,1)}), bf16[256,4,128]{2,1,0:T(4,128)(2,1)S(1)}, u32[]{:S(2)}, u32[]{:S(2)}) async-start(bf16[256,4,128]{2,1,0:T(4,128)(2,1)} %bitcast.5), calls=%async_computation | async-start | bytes 524288 | tf_op jit(solution)/shard_map/all_to_all | solution.py:114
  17.1 0.0 copy-start.2
  17.1 0.0 copy-done
  17.1 0.0 copy-done.1
  17.1 0.6 copy-done.2
  17.7 0.8 pack.1
  18.5 2.2 %collective-permute-start = (bf16[528,128]{1,0:T(8,128)(2,1)S(1)}, bf16[528,128]{1,0:T(8,128)(2,1)S(1)}, u32[]{:S(2)}, u32[]{:S(2)}) collective-permute-start(bf16[528,128]{1,0:T(8,128)(2,1)S(1)} %get-tuple-element.25), channel_id=1, source_target_pairs={{0,32},{4,36},{8,40},{12,44},{16,48},{20,52},{24,56},{28,60},{32,0... | collective-permute-start | bytes 405512 | tf_op jit(solution)/shard_map/ppermute | solution.py:120
  20.8 0.0 collective-permute-start.1
  20.8 1.6 %collective-permute-start.2 = (bf16[528,128]{1,0:T(8,128)(2,1)S(1)}, bf16[528,128]{1,0:T(8,128)(2,1)S(1)}, u32[]{:S(2)}, u32[]{:S(2)}) collective-permute-start(bf16[528,128]{1,0:T(8,128)(2,1)S(1)} %get-tuple-element.27), channel_id=1, source_target_pairs={{0,96},{4,100},{8,104},{12,108},{16,112},{20,116},{24,120},{28,124... | collective-permute-start | bytes 405512 | tf_op jit(solution)/shard_map/ppermute | solution.py:120
  22.3 2.8 %collective-permute-start.3 = (bf16[528,128]{1,0:T(8,128)(2,1)S(1)}, bf16[528,128]{1,0:T(8,128)(2,1)S(1)}, u32[]{:S(2)}, u32[]{:S(2)}) collective-permute-start(bf16[528,128]{1,0:T(8,128)(2,1)S(1)} %get-tuple-element.28), channel_id=1, source_target_pairs={{0,128},{4,132},{8,136},{12,140},{16,144},{20,148},{24,152},{28,15... | collective-permute-start | bytes 405512 | tf_op jit(solution)/shard_map/ppermute | solution.py:120
  25.1 2.1 %collective-permute-start.4 = (bf16[528,128]{1,0:T(8,128)(2,1)S(1)}, bf16[528,128]{1,0:T(8,128)(2,1)S(1)}, u32[]{:S(2)}, u32[]{:S(2)}) collective-permute-start(bf16[528,128]{1,0:T(8,128)(2,1)S(1)} %get-tuple-element.29), channel_id=1, source_target_pairs={{0,160},{4,164},{8,168},{12,172},{16,176},{20,180},{24,184},{28,18... | collective-permute-start | bytes 405512 | tf_op jit(solution)/shard_map/ppermute | solution.py:120
  27.9 0.0 collective-permute-done.refs_1_
  27.9 1.2 %collective-permute-start.5 = (bf16[528,128]{1,0:T(8,128)(2,1)S(1)}, bf16[528,128]{1,0:T(8,128)(2,1)S(1)}, u32[]{:S(2)}, u32[]{:S(2)}) collective-permute-start(bf16[528,128]{1,0:T(8,128)(2,1)S(1)} %get-tuple-element.30), channel_id=1, source_target_pairs={{0,192},{4,196},{8,200},{12,204},{16,208},{20,212},{24,216},{28,22... | collective-permute-start | bytes 405512 | tf_op jit(solution)/shard_map/ppermute | solution.py:120
  29.2 4.5 %collective-permute-done.1.refs_2_ = bf16[528,128]{1,0:T(8,128)(2,1)S(1)} collective-permute-done((bf16[528,128]{1,0:T(8,128)(2,1)S(1)}, bf16[528,128]{1,0:T(8,128)(2,1)S(1)}, u32[]{:S(2)}, u32[]{:S(2)}) %collective-permute-start.1) | collective-permute-done | bytes 135200 | tf_op jit(solution)/shard_map/ppermute | solution.py:120
  33.6 3.0 %collective-permute-start.6 = (bf16[528,128]{1,0:T(8,128)(2,1)S(1)}, bf16[528,128]{1,0:T(8,128)(2,1)S(1)}, u32[]{:S(2)}, u32[]{:S(2)}) collective-permute-start(bf16[528,128]{1,0:T(8,128)(2,1)S(1)} %get-tuple-element.31), channel_id=1, source_target_pairs={{0,224},{4,228},{8,232},{12,236},{16,240},{20,244},{24,248},{28,25... | collective-permute-start | bytes 405512 | tf_op jit(solution)/shard_map/ppermute | solution.py:120
  36.6 0.0 all-to-all-done
  36.6 0.2 fusion
  36.8 0.0 collective-permute-done.2.refs_3_
  36.8 1.6 %collective-permute-done.3.refs_4_ = bf16[528,128]{1,0:T(8,128)(2,1)S(1)} collective-permute-done((bf16[528,128]{1,0:T(8,128)(2,1)S(1)}, bf16[528,128]{1,0:T(8,128)(2,1)S(1)}, u32[]{:S(2)}, u32[]{:S(2)}) %collective-permute-start.3) | collective-permute-done | bytes 135200 | tf_op jit(solution)/shard_map/ppermute | solution.py:120
  38.5 0.0 collective-permute-done.4.refs_5_
  38.5 2.8 %collective-permute-done.5.refs_6_ = bf16[528,128]{1,0:T(8,128)(2,1)S(1)} collective-permute-done((bf16[528,128]{1,0:T(8,128)(2,1)S(1)}, bf16[528,128]{1,0:T(8,128)(2,1)S(1)}, u32[]{:S(2)}, u32[]{:S(2)}) %collective-permute-start.5) | collective-permute-done | bytes 135200 | tf_op jit(solution)/shard_map/ppermute | solution.py:120
  41.3 0.0 collective-permute-done.6.refs_7_
  41.3 8.9 %attention.1 = (bf16[512,128]{1,0:T(8,128)(2,1)S(1)}, bf16[512,128]{1,0:T(8,128)(2,1)S(1)}, bf16[512,128]{1,0:T(8,128)(2,1)S(1)}, bf16[512,128]{1,0:T(8,128)(2,1...) custom-call(f32[1]{0:T(128)} %bitcast.1.gate_ref, ...), custom_call_target="tpu_custom_call" | custom-call | tf_op jit(solution)/shard_map/attention/pallas_call | solution.py:135
  50.2 1.0 %pad_maximum_fusion = bf16[256,4,128]{2,1,0:T(4,128)(2,1)} fusion(bf16[256,2,128]{2,1,0:T(2,128)(2,1)S(1)} %bitcast.28, bf16[256,2,128]{2,1,0:T(2,128)(2,1)S(1)} %bitcast.27), kind=kLoop, calls=%fused_computation.1 | loop fusion | flops 524288 | bytes 524288 | tf_op jit(solution)/shard_map/concatenate | solution.py:150
  51.2 12.0 %all-to-all-start.1 = ((bf16[256,4,128]{2,1,0:T(4,128)(2,1)}), bf16[256,4,128]{2,1,0:T(4,128)(2,1)S(1)}, u32[]{:S(2)}, u32[]{:S(2)}) async-start(bf16[256,4,128]{2,1,0:T(4,128)(2,1)} %pad_maximum_fusion), calls=%async_computation.1 | async-start | bytes 524288 | tf_op jit(solution)/shard_map/all_to_all | solution.py:153
  63.3 2.2 %collective-permute-start.7 = (bf16[512,128]{1,0:T(8,128)(2,1)S(1)}, bf16[512,128]{1,0:T(8,128)(2,1)S(1)}, u32[]{:S(2)}, u32[]{:S(2)}) collective-permute-start(bf16[512,128]{1,0:T(8,128)(2,1)S(1)} %get-tuple-element.33), channel_id=1, source_target_pairs={{0,32},{4,36},{8,40},{12,44},{16,48},{20,52},{24,56},{28,60},{32,0... | collective-permute-start | bytes 393224 | tf_op jit(solution)/shard_map/ppermute | solution.py:120
  65.5 0.0 collective-permute-start.8
  65.5 1.6 %collective-permute-start.9 = (bf16[512,128]{1,0:T(8,128)(2,1)S(1)}, bf16[512,128]{1,0:T(8,128)(2,1)S(1)}, u32[]{:S(2)}, u32[]{:S(2)}) collective-permute-start(bf16[512,128]{1,0:T(8,128)(2,1)S(1)} %get-tuple-element.35), channel_id=1, source_target_pairs={{0,96},{4,100},{8,104},{12,108},{16,112},{20,116},{24,120},{28,124... | collective-permute-start | bytes 393224 | tf_op jit(solution)/shard_map/ppermute | solution.py:120
  67.1 2.8 %collective-permute-start.10 = (bf16[512,128]{1,0:T(8,128)(2,1)S(1)}, bf16[512,128]{1,0:T(8,128)(2,1)S(1)}, u32[]{:S(2)}, u32[]{:S(2)}) collective-permute-start(bf16[512,128]{1,0:T(8,128)(2,1)S(1)} %get-tuple-element.36), channel_id=1, source_target_pairs={{0,128},{4,132},{8,136},{12,140},{16,144},{20,148},{24,152},{28,15... | collective-permute-start | bytes 393224 | tf_op jit(solution)/shard_map/ppermute | solution.py:120
  69.8 2.1 %collective-permute-start.11 = (bf16[512,128]{1,0:T(8,128)(2,1)S(1)}, bf16[512,128]{1,0:T(8,128)(2,1)S(1)}, u32[]{:S(2)}, u32[]{:S(2)}) collective-permute-start(bf16[512,128]{1,0:T(8,128)(2,1)S(1)} %get-tuple-element.37), channel_id=1, source_target_pairs={{0,160},{4,164},{8,168},{12,172},{16,176},{20,180},{24,184},{28,18... | collective-permute-start | bytes 393224 | tf_op jit(solution)/shard_map/ppermute | solution.py:120
  72.0 0.0 collective-permute-done.7.refs_1_
  72.0 2.0 %collective-permute-start.12 = (bf16[512,128]{1,0:T(8,128)(2,1)S(1)}, bf16[512,128]{1,0:T(8,128)(2,1)S(1)}, u32[]{:S(2)}, u32[]{:S(2)}) collective-permute-start(bf16[512,128]{1,0:T(8,128)(2,1)S(1)} %get-tuple-element.38), channel_id=1, source_target_pairs={{0,192},{4,196},{8,200},{12,204},{16,208},{20,212},{24,216},{28,22... | collective-permute-start | bytes 393224 | tf_op jit(solution)/shard_map/ppermute | solution.py:120
  74.0 4.6 %collective-permute-done.8.refs_2_ = bf16[512,128]{1,0:T(8,128)(2,1)S(1)} collective-permute-done((bf16[512,128]{1,0:T(8,128)(2,1)S(1)}, bf16[512,128]{1,0:T(8,128)(2,1)S(1)}, u32[]{:S(2)}, u32[]{:S(2)}) %collective-permute-start.8) | collective-permute-done | bytes 131104 | tf_op jit(solution)/shard_map/ppermute | solution.py:120
  78.6 3.0 %collective-permute-start.13 = (bf16[512,128]{1,0:T(8,128)(2,1)S(1)}, bf16[512,128]{1,0:T(8,128)(2,1)S(1)}, u32[]{:S(2)}, u32[]{:S(2)}) collective-permute-start(bf16[512,128]{1,0:T(8,128)(2,1)S(1)} %get-tuple-element.39), channel_id=1, source_target_pairs={{0,224},{4,228},{8,232},{12,236},{16,240},{20,244},{24,248},{28,25... | collective-permute-start | bytes 393224 | tf_op jit(solution)/shard_map/ppermute | solution.py:120
  81.6 0.0 collective-permute-done.9.refs_3_
  81.6 1.5 %collective-permute-done.10.refs_4_ = bf16[512,128]{1,0:T(8,128)(2,1)S(1)} collective-permute-done((bf16[512,128]{1,0:T(8,128)(2,1)S(1)}, bf16[512,128]{1,0:T(8,128)(2,1)S(1)}, u32[]{:S(2)}, u32[]{:S(2)}) %collective-permute-start.10) | collective-permute-done | bytes 131104 | tf_op jit(solution)/shard_map/ppermute | solution.py:120
  83.2 0.0 collective-permute-done.11.refs_5_
  83.2 1.2 %collective-permute-done.12.refs_6_ = bf16[512,128]{1,0:T(8,128)(2,1)S(1)} collective-permute-done((bf16[512,128]{1,0:T(8,128)(2,1)S(1)}, bf16[512,128]{1,0:T(8,128)(2,1)S(1)}, u32[]{:S(2)}, u32[]{:S(2)}) %collective-permute-start.12) | collective-permute-done | bytes 131104 | tf_op jit(solution)/shard_map/ppermute | solution.py:120
  84.3 1.4 %collective-permute-done.13.refs_7_ = bf16[512,128]{1,0:T(8,128)(2,1)S(1)} collective-permute-done((bf16[512,128]{1,0:T(8,128)(2,1)S(1)}, bf16[512,128]{1,0:T(8,128)(2,1)S(1)}, u32[]{:S(2)}, u32[]{:S(2)}) %collective-permute-start.13) | collective-permute-done | bytes 131104 | tf_op jit(solution)/shard_map/ppermute | solution.py:120
  85.7 1.3 %unpack.1 = (bf16[256,1024]{1,0:T(8,128)(2,1)}, bf16[256,1024]{1,0:T(8,128)(2,1)}) custom-call(s32[1]{0:T(128)} %bitcast.place_ref, bf16[512,128]{1,0:T(8,128)(2,1)S(1)} %get-tuple-element.32.refs_0_, bf16[512,128]{1,0:T(8,128)(2,1)S(1)} %collective-permute-done.7.refs_1_, bf16[512,128]{1,0:T(8,128)(2,1)S(1)} %collective-permute-done.8.refs_2_, ...), custom_call_target="tpu_custom_call" | custom-call | tf_op jit(solution)/shard_map/unpack/pallas_call | solution.py:156
  87.0 0.0 all-to-all-done.1
  87.0 0.1 convert_reduce_fusion
  87.2 0.6 copy.21
  87.8 0.6 copy.22
  (4 shorter events, 0.1 us)
Async XLA Ops:
  0.6 16.5 %copy-start = (bf16[256,1024]{1,0:T(8,128)(2,1)S(1)}, bf16[256,1024]{1,0:T(8,128)(2,1)}, u32[]{:S(2)}) copy-start(bf16[256,1024]{1,0:T(8,128)(2,1)} %q_ref.1) | copy-start | bytes 1572868
  0.6 16.5 %copy-start.1 = (bf16[256,1024]{1,0:T(8,128)(2,1)S(1)}, bf16[256,1024]{1,0:T(8,128)(2,1)}, u32[]{:S(2)}) copy-start(bf16[256,1024]{1,0:T(8,128)(2,1)} %c_ref.1) | copy-start | bytes 1572868
  2.4 34.3 %all-to-all-start = ((bf16[256,4,128]{2,1,0:T(4,128)(2,1)}), bf16[256,4,128]{2,1,0:T(4,128)(2,1)S(1)}, u32[]{:S(2)}, u32[]{:S(2)}) async-start(bf16[256,4,128]{2,1,0:T(4,128)(2,1)} %bitcast.5), calls=%async_computation | async-start | bytes 524288 | tf_op jit(solution)/shard_map/all_to_all | solution.py:114
  17.1 0.7 copy-start.2
  18.5 9.4 %collective-permute-start = (bf16[528,128]{1,0:T(8,128)(2,1)S(1)}, bf16[528,128]{1,0:T(8,128)(2,1)S(1)}, u32[]{:S(2)}, u32[]{:S(2)}) collective-permute-start(bf16[528,128]{1,0:T(8,128)(2,1)S(1)} %get-tuple-element.25), channel_id=1, source_target_pairs={{0,32},{4,36},{8,40},{12,44},{16,48},{20,52},{24,56},{28,60},{32,0... | collective-permute-start | bytes 405512 | tf_op jit(solution)/shard_map/ppermute | solution.py:120
  20.8 12.9 %collective-permute-start.1 = (bf16[528,128]{1,0:T(8,128)(2,1)S(1)}, bf16[528,128]{1,0:T(8,128)(2,1)S(1)}, u32[]{:S(2)}, u32[]{:S(2)}) collective-permute-start(bf16[528,128]{1,0:T(8,128)(2,1)S(1)} %get-tuple-element.26), channel_id=1, source_target_pairs={{0,64},{4,68},{8,72},{12,76},{16,80},{20,84},{24,88},{28,92},{32,9... | collective-permute-start | bytes 405512 | tf_op jit(solution)/shard_map/ppermute | solution.py:120
  20.8 16.1 %collective-permute-start.2 = (bf16[528,128]{1,0:T(8,128)(2,1)S(1)}, bf16[528,128]{1,0:T(8,128)(2,1)S(1)}, u32[]{:S(2)}, u32[]{:S(2)}) collective-permute-start(bf16[528,128]{1,0:T(8,128)(2,1)S(1)} %get-tuple-element.27), channel_id=1, source_target_pairs={{0,96},{4,100},{8,104},{12,108},{16,112},{20,116},{24,120},{28,124... | collective-permute-start | bytes 405512 | tf_op jit(solution)/shard_map/ppermute | solution.py:120
  22.3 16.1 %collective-permute-start.3 = (bf16[528,128]{1,0:T(8,128)(2,1)S(1)}, bf16[528,128]{1,0:T(8,128)(2,1)S(1)}, u32[]{:S(2)}, u32[]{:S(2)}) collective-permute-start(bf16[528,128]{1,0:T(8,128)(2,1)S(1)} %get-tuple-element.28), channel_id=1, source_target_pairs={{0,128},{4,132},{8,136},{12,140},{16,144},{20,148},{24,152},{28,15... | collective-permute-start | bytes 405512 | tf_op jit(solution)/shard_map/ppermute | solution.py:120
  25.1 13.4 %collective-permute-start.4 = (bf16[528,128]{1,0:T(8,128)(2,1)S(1)}, bf16[528,128]{1,0:T(8,128)(2,1)S(1)}, u32[]{:S(2)}, u32[]{:S(2)}) collective-permute-start(bf16[528,128]{1,0:T(8,128)(2,1)S(1)} %get-tuple-element.29), channel_id=1, source_target_pairs={{0,160},{4,164},{8,168},{12,172},{16,176},{20,180},{24,184},{28,18... | collective-permute-start | bytes 405512 | tf_op jit(solution)/shard_map/ppermute | solution.py:120
  27.9 13.4 %collective-permute-start.5 = (bf16[528,128]{1,0:T(8,128)(2,1)S(1)}, bf16[528,128]{1,0:T(8,128)(2,1)S(1)}, u32[]{:S(2)}, u32[]{:S(2)}) collective-permute-start(bf16[528,128]{1,0:T(8,128)(2,1)S(1)} %get-tuple-element.30), channel_id=1, source_target_pairs={{0,192},{4,196},{8,200},{12,204},{16,208},{20,212},{24,216},{28,22... | collective-permute-start | bytes 405512 | tf_op jit(solution)/shard_map/ppermute | solution.py:120
  33.6 7.7 %collective-permute-start.6 = (bf16[528,128]{1,0:T(8,128)(2,1)S(1)}, bf16[528,128]{1,0:T(8,128)(2,1)S(1)}, u32[]{:S(2)}, u32[]{:S(2)}) collective-permute-start(bf16[528,128]{1,0:T(8,128)(2,1)S(1)} %get-tuple-element.31), channel_id=1, source_target_pairs={{0,224},{4,228},{8,232},{12,236},{16,240},{20,244},{24,248},{28,25... | collective-permute-start | bytes 405512 | tf_op jit(solution)/shard_map/ppermute | solution.py:120
  51.2 35.8 %all-to-all-start.1 = ((bf16[256,4,128]{2,1,0:T(4,128)(2,1)}), bf16[256,4,128]{2,1,0:T(4,128)(2,1)S(1)}, u32[]{:S(2)}, u32[]{:S(2)}) async-start(bf16[256,4,128]{2,1,0:T(4,128)(2,1)} %pad_maximum_fusion), calls=%async_computation.1 | async-start | bytes 524288 | tf_op jit(solution)/shard_map/all_to_all | solution.py:153
  63.3 8.7 %collective-permute-start.7 = (bf16[512,128]{1,0:T(8,128)(2,1)S(1)}, bf16[512,128]{1,0:T(8,128)(2,1)S(1)}, u32[]{:S(2)}, u32[]{:S(2)}) collective-permute-start(bf16[512,128]{1,0:T(8,128)(2,1)S(1)} %get-tuple-element.33), channel_id=1, source_target_pairs={{0,32},{4,36},{8,40},{12,44},{16,48},{20,52},{24,56},{28,60},{32,0... | collective-permute-start | bytes 393224 | tf_op jit(solution)/shard_map/ppermute | solution.py:120
  65.5 13.1 %collective-permute-start.8 = (bf16[512,128]{1,0:T(8,128)(2,1)S(1)}, bf16[512,128]{1,0:T(8,128)(2,1)S(1)}, u32[]{:S(2)}, u32[]{:S(2)}) collective-permute-start(bf16[512,128]{1,0:T(8,128)(2,1)S(1)} %get-tuple-element.34), channel_id=1, source_target_pairs={{0,64},{4,68},{8,72},{12,76},{16,80},{20,84},{24,88},{28,92},{32,9... | collective-permute-start | bytes 393224 | tf_op jit(solution)/shard_map/ppermute | solution.py:120
  65.5 16.1 %collective-permute-start.9 = (bf16[512,128]{1,0:T(8,128)(2,1)S(1)}, bf16[512,128]{1,0:T(8,128)(2,1)S(1)}, u32[]{:S(2)}, u32[]{:S(2)}) collective-permute-start(bf16[512,128]{1,0:T(8,128)(2,1)S(1)} %get-tuple-element.35), channel_id=1, source_target_pairs={{0,96},{4,100},{8,104},{12,108},{16,112},{20,116},{24,120},{28,124... | collective-permute-start | bytes 393224 | tf_op jit(solution)/shard_map/ppermute | solution.py:120
  67.1 16.1 %collective-permute-start.10 = (bf16[512,128]{1,0:T(8,128)(2,1)S(1)}, bf16[512,128]{1,0:T(8,128)(2,1)S(1)}, u32[]{:S(2)}, u32[]{:S(2)}) collective-permute-start(bf16[512,128]{1,0:T(8,128)(2,1)S(1)} %get-tuple-element.36), channel_id=1, source_target_pairs={{0,128},{4,132},{8,136},{12,140},{16,144},{20,148},{24,152},{28,15... | collective-permute-start | bytes 393224 | tf_op jit(solution)/shard_map/ppermute | solution.py:120
  69.8 13.3 %collective-permute-start.11 = (bf16[512,128]{1,0:T(8,128)(2,1)S(1)}, bf16[512,128]{1,0:T(8,128)(2,1)S(1)}, u32[]{:S(2)}, u32[]{:S(2)}) collective-permute-start(bf16[512,128]{1,0:T(8,128)(2,1)S(1)} %get-tuple-element.37), channel_id=1, source_target_pairs={{0,160},{4,164},{8,168},{12,172},{16,176},{20,180},{24,184},{28,18... | collective-permute-start | bytes 393224 | tf_op jit(solution)/shard_map/ppermute | solution.py:120
  72.0 12.4 %collective-permute-start.12 = (bf16[512,128]{1,0:T(8,128)(2,1)S(1)}, bf16[512,128]{1,0:T(8,128)(2,1)S(1)}, u32[]{:S(2)}, u32[]{:S(2)}) collective-permute-start(bf16[512,128]{1,0:T(8,128)(2,1)S(1)} %get-tuple-element.38), channel_id=1, source_target_pairs={{0,192},{4,196},{8,200},{12,204},{16,208},{20,212},{24,216},{28,22... | collective-permute-start | bytes 393224 | tf_op jit(solution)/shard_map/ppermute | solution.py:120
  78.6 7.1 %collective-permute-start.13 = (bf16[512,128]{1,0:T(8,128)(2,1)S(1)}, bf16[512,128]{1,0:T(8,128)(2,1)S(1)}, u32[]{:S(2)}, u32[]{:S(2)}) collective-permute-start(bf16[512,128]{1,0:T(8,128)(2,1)S(1)} %get-tuple-element.39), channel_id=1, source_target_pairs={{0,224},{4,228},{8,232},{12,236},{16,240},{20,244},{24,248},{28,25... | collective-permute-start | bytes 393224 | tf_op jit(solution)/shard_map/ppermute | solution.py:120

commit v2 on v1

v2 whole, which is shorter than its diff:
```python
import functools
import math

import jax
import jax.numpy as jnp
from jax import lax
from jax.experimental import pallas as pl
from jax.experimental.pallas import tpu as pltpu
from jax.sharding import Mesh, PartitionSpec as P

DH = 128
TBLK = 128
BLOCKS = 2
GROUP = 4
HALVES = 2
ZSIZE = 8
TP = 4
SIZES = {"h": HALVES, "g": GROUP, "z": ZSIZE, "tp": TP}
AXES = tuple(SIZES)
ORDER = ("h", "g", "z", "tp")
UNPACK = 0
EXTRA = 16

masked_fill = -1e30
SCALE = 1.0 / DH**0.5
LOG2E = math.log2(math.e)
PARAMS = pltpu.CompilerParams(vmem_limit_bytes=32 * 2**20)
SMEM = pl.BlockSpec(memory_space=pltpu.SMEM)
VMEM = pl.BlockSpec(memory_space=pltpu.VMEM)


def stride(axis):
    return math.prod(SIZES[a] for a in ORDER[ORDER.index(axis) + 1 :])


def source(**at):
    return sum(i * stride(axis) for axis, i in at.items())


def pack_kernel(place_ref, last_ref, q_ref, c_ref, *out_refs):
    tok, width = q_ref.shape[0], out_refs[0].shape[1]
    half = EXTRA // 2
    rows = lax.broadcasted_iota(jnp.int32, (EXTRA, width), 0)
    frames = jnp.where(rows < half, last_ref[0], last_ref[1])
    frames = frames.astype(jnp.float32).astype(jnp.bfloat16)
    for k, out in enumerate(out_refs):
        cols = pl.ds(pl.multiple_of((place_ref[0] ^ k) * width, width), width)
        out[0:tok, :] = q_ref[:, cols]
        out[tok : 2 * tok, :] = c_ref[:, cols]
        out[2 * tok : 2 * tok + EXTRA, :] = frames


def unpack_kernel(place_ref, *refs):
    block_refs, (att_ref, dq_ref) = refs[:GROUP], refs[GROUP:]
    tok, width = att_ref.shape[0], block_refs[0].shape[1]
    for k, block in enumerate(block_refs):
        cols = pl.ds(pl.multiple_of((place_ref[0] ^ k) * width, width), width)
        att_ref[:, cols] = block[0:tok, :]
        dq_ref[:, cols] = block[tok : 2 * tok, :]


def settle_kernel(in_ref, k_ref, v_ref):
    own, wide = k_ref.shape
    width = in_ref.shape[2]
    for g in range(GROUP):
        for t in range(TP):
            total = jnp.zeros((2 * own, width), jnp.float32)
            for h in range(HALVES):
                for z in range(ZSIZE):
                    total += in_ref[source(h=h, g=g, z=z, tp=t)].astype(jnp.float32)
            col = (t * GROUP + g) * width
            k_ref[:, col : col + width] = total[0:own]
            v_ref[:, col : col + width] = total[own:]


def dot(a, b, dims):
    return lax.dot_general(a, b, (dims, ((), ())), preferred_element_type=jnp.float32)


def attention_kernel(gate_ref, kv_ref, *refs):
    msgs, outs = refs[:GROUP], refs[GROUP : 2 * GROUP]
    grad_ref, k_s, v_s, dk_s, dv_s = refs[2 * GROUP :]
    tok = outs[0].shape[0] // 2
    lat, width = k_s.shape
    own = kv_ref.shape[1] // 2
    gate = gate_ref[0]
    k_s[...] = kv_ref[:, 0:own, :].reshape(lat, width)
    v_s[...] = kv_ref[:, own : 2 * own, :].reshape(lat, width)
    place = lax.broadcasted_iota(jnp.int32, (1, lat), 1) // own
    frame = place // stride("h") % HALVES * GROUP + place // stride("g") % GROUP
    frame = frame.astype(jnp.float32)

    def bias(msg, i):
        row = 2 * tok + i * (EXTRA // 2)
        last = msg[row : row + 1, 0:DH].astype(jnp.float32)
        return jnp.where(frame <= jnp.concatenate([last] * (lat // DH), axis=1), 0.0, masked_fill)

    def step(first):
        blocks = range(first, first + BLOCKS)
        biases = [bias(msgs[j], i) for j in blocks for i in range(tok // TBLK)]
        heads = []
        for h in range(width // DH):
            cols = slice(h * DH, (h + 1) * DH)
            q = jnp.concatenate([msgs[j][0:tok, cols] for j in blocks], axis=0)
            cot = jnp.concatenate([msgs[j][tok : 2 * tok, cols] for j in blocks], axis=0)
            gcot = (gate * cot.astype(jnp.float32)).astype(jnp.bfloat16)
            heads.append((cols, q, gcot, k_s[:, cols], v_s[:, cols]))

        def softmax(head):
            _, q, _, keys, _ = head
            scores = dot(q, keys, ((1,), (1,)))
            parts = [
                scores[i * TBLK : (i + 1) * TBLK] * (SCALE * LOG2E) + b for i, b in enumerate(biases)
            ]
            scores = jnp.concatenate(parts, axis=0)
            expo = jnp.exp2(scores - jnp.max(scores, axis=-1, keepdims=True))
            return expo * (1.0 / jnp.sum(expo, axis=-1, keepdims=True))

        def prob_grads(head):
            _, _, gcot, _, values = head
            return dot(gcot, values, ((1,), (1,)))

        def score_grads(weights, grads):
            inner = jnp.sum(weights * grads, axis=-1, keepdims=True)
            return (weights * (grads - inner)).astype(jnp.bfloat16)

        def finish(head, low, sgrad):
            cols, q, gcot, keys, values = head
            out = (gate * dot(low, values, ((1,), (0,)))).astype(jnp.bfloat16)
            for i, j in enumerate(blocks):
                outs[j][0:tok, cols] = out[i * tok : (i + 1) * tok]
            out = (SCALE * dot(sgrad, keys, ((1,), (0,)))).astype(jnp.bfloat16)
            for i, j in enumerate(blocks):
                outs[j][tok : 2 * tok, cols] = out[i * tok : (i + 1) * tok]
            dk = dot(sgrad, q, ((0,), (0,)))
            dv = dot(low, gcot, ((0,), (0,)))
            dk_s[:, cols] = dk if first == 0 else dk_s[:, cols] + dk
            dv_s[:, cols] = dv if first == 0 else dv_s[:, cols] + dv

        one, two = heads
        weights1, grads1 = softmax(one), prob_grads(one)
        weights2 = softmax(two)
        low1, sgrad1 = weights1.astype(jnp.bfloat16), score_grads(weights1, grads1)
        grads2 = prob_grads(two)
        finish(one, low1, sgrad1)
        low2, sgrad2 = weights2.astype(jnp.bfloat16), score_grads(weights2, grads2)
        finish(two, low2, sgrad2)

    for first in range(0, GROUP, BLOCKS):
        step(first)
    for i, grads in enumerate((SCALE * dk_s[...], dv_s[...])):
        piece = grads.astype(jnp.bfloat16).reshape(lat // own, own, width)
        grad_ref[:, i * own : (i + 1) * own, :] = piece


def cut_kernel(k_ref, v_ref, out_ref):
    width = out_ref.shape[2]
    for t in range(TP):
        for g in range(GROUP):
            col = (t * GROUP + g) * width
            piece = jnp.concatenate([k_ref[:, col : col + width], v_ref[:, col : col + width]], axis=0)
            for h in range(HALVES):
                for z in range(ZSIZE):
                    out_ref[source(h=h, g=g, z=z, tp=t)] = piece


def call(kernel, shapes, specs, *args, cost=0, **kwargs):
    if cost:
        kwargs["cost_estimate"] = pl.CostEstimate(flops=cost, bytes_accessed=0, transcendentals=0)
    name = kernel.__name__.removesuffix("_kernel")
    out_specs = [VMEM] * len(shapes)
    return pl.pallas_call(
        kernel,
        out_shape=shapes,
        in_specs=specs,
        out_specs=out_specs,
        compiler_params=PARAMS,
        name=name,
        **kwargs,
    )(*args)


def swap(x, axis, size, k):
    return x if k == 0 else lax.ppermute(x, axis, [(i, i ^ k) for i in range(size)])


def per_device(queries, latent_keys, latent_values, gate_logit, last_frame, cotangent):
    tok, columns = queries.shape
    own, wide = latent_keys.shape
    width = columns // GROUP
    devices = HALVES * GROUP * ZSIZE * TP
    lat = own * devices
    place = lax.axis_index("g").astype(jnp.int32).reshape(1)
    gate = jnp.tanh(gate_logit).astype(jnp.float32).reshape(1)

    def low(*shape):
        return jax.ShapeDtypeStruct(shape, jnp.bfloat16)

    (both,) = call(
        cut_kernel, [low(devices, 2 * own, width)], [VMEM] * 2, latent_keys, latent_values
    )
    both = lax.all_to_all(both, ORDER, 0, 0)

    msgs = call(
        pack_kernel,
        [low(2 * tok + EXTRA, width)] * GROUP,
        [SMEM, SMEM, VMEM, VMEM],
        place,
        last_frame,
        queries,
        cotangent,
    )
    msgs = [swap(x, "g", GROUP, k) for k, x in enumerate(msgs)]

    *backs, terms = call(
        attention_kernel,
        [low(2 * tok, width)] * GROUP + [low(devices, 2 * own, width)],
        [SMEM] + [VMEM] * (1 + GROUP),
        gate,
        both,
        *msgs,
        scratch_shapes=[
            pltpu.VMEM((lat, width), jnp.bfloat16),
            pltpu.VMEM((lat, width), jnp.bfloat16),
            pltpu.VMEM((lat, width), jnp.float32),
            pltpu.VMEM((lat, width), jnp.float32),
        ],
    )

    terms = lax.all_to_all(terms, ORDER, 0, 0)
    grad = jax.ShapeDtypeStruct((own, wide), jnp.float32)
    key_grad, value_grad = call(settle_kernel, [grad] * 2, [VMEM], terms)

    backs = [swap(x, "g", GROUP, k) for k, x in enumerate(backs)]
    attended, query_grad = call(
        unpack_kernel, [low(tok, columns)] * 2, [SMEM] + [VMEM] * GROUP, place, *backs, cost=UNPACK
    )
    return (attended, query_grad, key_grad, value_grad)


def solution(mesh):
    fine = Mesh(mesh.devices.reshape(tuple(SIZES.values())), AXES)
    tokens = P(AXES[:3], "tp")
    rows = P(AXES, None)
    return jax.shard_map(
        per_device,
        mesh=fine,
        in_specs=(tokens, rows, rows, P(), P(AXES[:3]), tokens),
        out_specs=(tokens, tokens, rows, rows),
        check_vma=False,
    )
```

time: 88.7 us -> 79.3 us (0.89)
  the two profiles are of different devices: /device:TPU:2 before, /device:TPU:1 now
where the time goes in v2:
time: 79.3 us; the launch traced here: 78.9 us
  waiting for transfers between devices  33.6 us (42%)
  starting transfers between devices  33.2 us (42%)
  Pallas kernels  8.57 us (11%)
  local copies, waits for them, and re-layouts  2.07 us (3%)
  between operations  1.39 us (2%)
    ppermute x6, waiting for transfers between devices, swap(): lax.ppermute(x, axis, [(i, i ^ k) for i in range(size)])  32.8 us
    all_to_all x1, starting transfers between devices, per_device(): both = lax.all_to_all(both, ORDER, 0, 0)  15.7 us
    all_to_all x1, starting transfers between devices, per_device(): terms = lax.all_to_all(terms, ORDER, 0, 0)  12.1 us
    pallas_call x5, Pallas kernels, call(): pl.pallas_call(kernel, out_shape=shapes, in_specs=specs, out_specs=out_sp...  8.57 us
    ppermute x6, starting transfers between devices, swap(): lax.ppermute(x, axis, [(i, i ^ k) for i in range(size)])  5.51 us
    unnamed x10, local copies, waits for them, and re-layouts  2.07 us
  transfers between devices with their start and end apart: 8, of which 8 were waited for; matrix products, arithmetic and copies ran while one was open for 0% of the time, Pallas kernels for 2%

profile of v2, /device:TPU:1, one launch (start us, length us, event | category | flops | bytes accessed | tf_op | source)
XLA Modules:
  0.0 78.9 jit_solution(18288773729431804662)
XLA Ops:
  0.6 0.0 copy-start.2
  0.6 0.7 copy-done.2
  1.3 0.0 copy-start.3
  1.4 0.7 copy-done.3
  2.1 0.9 %cut.1 = bf16[256,4,256]{2,1,0:T(4,128)(2,1)} custom-call(bf16[2,4096]{1,0:T(2,128)(2,1)S(1)} %copy-done.2, bf16[2,4096]{1,0:T(2,128)(2,1)S(1)} %copy-done.3), custom_call_target="tpu_custom_call" | custom-call | tf_op jit(solution)/shard_map/cut/pallas_call | solution.py:172
  3.0 0.0 copy-start
  3.0 0.0 copy-start.1
  3.0 15.7 %all-to-all-start = ((bf16[256,4,256]{2,1,0:T(4,128)(2,1)}), bf16[256,4,256]{2,1,0:T(4,128)(2,1)S(1)}, u32[]{:S(2)}, u32[]{:S(2)}) async-start(bf16[256,4,256]{2,1,0:T(4,128)(2,1)} %cut.1), calls=%async_computation | async-start | bytes 1048576 | tf_op jit(solution)/shard_map/all_to_all | solution.py:202
  18.7 0.0 copy-start.4
  18.7 0.0 copy-done
  18.7 0.0 copy-done.1
  18.7 0.6 copy-done.4
  19.3 0.7 pack.1
  20.0 1.5 %collective-permute-start = (bf16[528,256]{1,0:T(8,128)(2,1)S(1)}, bf16[528,256]{1,0:T(8,128)(2,1)S(1)}, u32[]{:S(2)}, u32[]{:S(2)}) collective-permute-start(bf16[528,256]{1,0:T(8,128)(2,1)S(1)} %get-tuple-element.18), channel_id=1, source_target_pairs={{0,32},{32,0},{64,96},{96,64},{1,33},{33,1},{65,97},{97,65},{2,34}... | collective-permute-start | bytes 811016 | tf_op jit(solution)/shard_map/ppermute | solution.py:184
  21.5 1.2 %collective-permute-start.1 = (bf16[528,256]{1,0:T(8,128)(2,1)S(1)}, bf16[528,256]{1,0:T(8,128)(2,1)S(1)}, u32[]{:S(2)}, u32[]{:S(2)}) collective-permute-start(bf16[528,256]{1,0:T(8,128)(2,1)S(1)} %get-tuple-element.19), channel_id=1, source_target_pairs={{0,64},{32,96},{64,0},{96,32},{1,65},{33,97},{65,1},{97,33},{2,66}... | collective-permute-start | bytes 811016 | tf_op jit(solution)/shard_map/ppermute | solution.py:184
  22.7 0.1 collective-permute-start.2
  23.5 7.0 %collective-permute-done.refs_1_ = bf16[528,256]{1,0:T(8,128)(2,1)S(1)} collective-permute-done((bf16[528,256]{1,0:T(8,128)(2,1)S(1)}, bf16[528,256]{1,0:T(8,128)(2,1)S(1)}, u32[]{:S(2)}, u32[]{:S(2)}) %collective-permute-start) | collective-permute-done | bytes 270368 | tf_op jit(solution)/shard_map/ppermute | solution.py:184
  30.5 3.3 %collective-permute-done.1.refs_2_ = bf16[528,256]{1,0:T(8,128)(2,1)S(1)} collective-permute-done((bf16[528,256]{1,0:T(8,128)(2,1)S(1)}, bf16[528,256]{1,0:T(8,128)(2,1)S(1)}, u32[]{:S(2)}, u32[]{:S(2)}) %collective-permute-start.1) | collective-permute-done | bytes 270368 | tf_op jit(solution)/shard_map/ppermute | solution.py:184
  33.8 5.7 %collective-permute-done.2.refs_3_ = bf16[528,256]{1,0:T(8,128)(2,1)S(1)} collective-permute-done((bf16[528,256]{1,0:T(8,128)(2,1)S(1)}, bf16[528,256]{1,0:T(8,128)(2,1)S(1)}, u32[]{:S(2)}, u32[]{:S(2)}) %collective-permute-start.2) | collective-permute-done | bytes 270368 | tf_op jit(solution)/shard_map/ppermute | solution.py:184
  39.5 0.3 all-to-all-done.kv_ref
  39.8 5.1 %attention.1 = (bf16[512,256]{1,0:T(8,128)(2,1)S(1)}, bf16[512,256]{1,0:T(8,128)(2,1)S(1)}, bf16[512,256]{1,0:T(8,128)(2,1)S(1)}, bf16[512,256]{1,0:T(8,128)(2,1)S(1)}, bf16[256,4,256]{2,1,0:T(4,128)(2,1)}) custom-call(f32[1]{0:T(128)} %bitcast.1.gate_ref, bf16[256,4,256]{2,1,0:T(4,128)(2,1)S(1)} %all-to-all-done.kv_ref, ...), custom_call_target="tpu_custom_call" | custom-call | tf_op jit(solution)/shard_map/attention/pallas_call | solution.py:172
  45.0 12.1 %all-to-all-start.1 = ((bf16[256,4,256]{2,1,0:T(4,128)(2,1)}), bf16[256,4,256]{2,1,0:T(4,128)(2,1)S(1)}, u32[]{:S(2)}, u32[]{:S(2)}) async-start(bf16[256,4,256]{2,1,0:T(4,128)(2,1)} %get-tuple-element.27), calls=%async_computation.1 | async-start | bytes 1048576 | tf_op jit(solution)/shard_map/all_to_all | solution.py:230
  57.0 1.5 %collective-permute-start.3 = (bf16[512,256]{1,0:T(8,128)(2,1)S(1)}, bf16[512,256]{1,0:T(8,128)(2,1)S(1)}, u32[]{:S(2)}, u32[]{:S(2)}) collective-permute-start(bf16[512,256]{1,0:T(8,128)(2,1)S(1)} %get-tuple-element.22), channel_id=1, source_target_pairs={{0,32},{32,0},{64,96},{96,64},{1,33},{33,1},{65,97},{97,65},{2,34}... | collective-permute-start | bytes 786440 | tf_op jit(solution)/shard_map/ppermute | solution.py:184
  58.5 1.2 %collective-permute-start.4 = (bf16[512,256]{1,0:T(8,128)(2,1)S(1)}, bf16[512,256]{1,0:T(8,128)(2,1)S(1)}, u32[]{:S(2)}, u32[]{:S(2)}) collective-permute-start(bf16[512,256]{1,0:T(8,128)(2,1)S(1)} %get-tuple-element.23), channel_id=1, source_target_pairs={{0,64},{32,96},{64,0},{96,32},{1,65},{33,97},{65,1},{97,33},{2,66}... | collective-permute-start | bytes 786440 | tf_op jit(solution)/shard_map/ppermute | solution.py:184
  59.7 0.1 collective-permute-start.5
  59.8 7.7 %collective-permute-done.3.refs_1_ = bf16[512,256]{1,0:T(8,128)(2,1)S(1)} collective-permute-done((bf16[512,256]{1,0:T(8,128)(2,1)S(1)}, bf16[512,256]{1,0:T(8,128)(2,1)S(1)}, u32[]{:S(2)}, u32[]{:S(2)}) %collective-permute-start.3) | collective-permute-done | bytes 262176 | tf_op jit(solution)/shard_map/ppermute | solution.py:184
  67.5 3.3 %collective-permute-done.4.refs_2_ = bf16[512,256]{1,0:T(8,128)(2,1)S(1)} collective-permute-done((bf16[512,256]{1,0:T(8,128)(2,1)S(1)}, bf16[512,256]{1,0:T(8,128)(2,1)S(1)}, u32[]{:S(2)}, u32[]{:S(2)}) %collective-permute-start.4) | collective-permute-done | bytes 262176 | tf_op jit(solution)/shard_map/ppermute | solution.py:184
  70.8 5.7 %collective-permute-done.5.refs_3_ = bf16[512,256]{1,0:T(8,128)(2,1)S(1)} collective-permute-done((bf16[512,256]{1,0:T(8,128)(2,1)S(1)}, bf16[512,256]{1,0:T(8,128)(2,1)S(1)}, u32[]{:S(2)}, u32[]{:S(2)}) %collective-permute-start.5) | collective-permute-done | bytes 262176 | tf_op jit(solution)/shard_map/ppermute | solution.py:184
  76.5 1.1 %unpack.1 = (bf16[256,1024]{1,0:T(8,128)(2,1)}, bf16[256,1024]{1,0:T(8,128)(2,1)}) custom-call(s32[1]{0:T(128)} %bitcast.place_ref, bf16[512,256]{1,0:T(8,128)(2,1)S(1)} %get-tuple-element.21.refs_0_, bf16[512,256]{1,0:T(8,128)(2,1)S(1)} %collective-permute-done.3.refs_1_, bf16[512,256]{1,0:T(8,128)(2,1)S(1)} %collective-permute-done.4.refs_2_, ...), custom_call_target="tpu_custom_call" | custom-call | tf_op jit(solution)/shard_map/unpack/pallas_call | solution.py:172
  77.6 0.6 all-to-all-done.1.in_ref
  78.2 0.7 settle.1
Async XLA Ops:
  0.6 0.7 copy-start.2
  1.3 0.7 copy-start.3
  3.0 15.7 %copy-start = (bf16[256,1024]{1,0:T(8,128)(2,1)S(1)}, bf16[256,1024]{1,0:T(8,128)(2,1)}, u32[]{:S(2)}) copy-start(bf16[256,1024]{1,0:T(8,128)(2,1)} %q_ref.1) | copy-start | bytes 1572868
  3.0 15.7 %copy-start.1 = (bf16[256,1024]{1,0:T(8,128)(2,1)S(1)}, bf16[256,1024]{1,0:T(8,128)(2,1)}, u32[]{:S(2)}) copy-start(bf16[256,1024]{1,0:T(8,128)(2,1)} %c_ref.1) | copy-start | bytes 1572868
  3.0 36.8 %all-to-all-start = ((bf16[256,4,256]{2,1,0:T(4,128)(2,1)}), bf16[256,4,256]{2,1,0:T(4,128)(2,1)S(1)}, u32[]{:S(2)}, u32[]{:S(2)}) async-start(bf16[256,4,256]{2,1,0:T(4,128)(2,1)} %cut.1), calls=%async_computation | async-start | bytes 1048576 | tf_op jit(solution)/shard_map/all_to_all | solution.py:202
  18.7 0.7 copy-start.4
  20.0 10.5 %collective-permute-start = (bf16[528,256]{1,0:T(8,128)(2,1)S(1)}, bf16[528,256]{1,0:T(8,128)(2,1)S(1)}, u32[]{:S(2)}, u32[]{:S(2)}) collective-permute-start(bf16[528,256]{1,0:T(8,128)(2,1)S(1)} %get-tuple-element.18), channel_id=1, source_target_pairs={{0,32},{32,0},{64,96},{96,64},{1,33},{33,1},{65,97},{97,65},{2,34}... | collective-permute-start | bytes 811016 | tf_op jit(solution)/shard_map/ppermute | solution.py:184
  21.5 12.3 %collective-permute-start.1 = (bf16[528,256]{1,0:T(8,128)(2,1)S(1)}, bf16[528,256]{1,0:T(8,128)(2,1)S(1)}, u32[]{:S(2)}, u32[]{:S(2)}) collective-permute-start(bf16[528,256]{1,0:T(8,128)(2,1)S(1)} %get-tuple-element.19), channel_id=1, source_target_pairs={{0,64},{32,96},{64,0},{96,32},{1,65},{33,97},{65,1},{97,33},{2,66}... | collective-permute-start | bytes 811016 | tf_op jit(solution)/shard_map/ppermute | solution.py:184
  22.7 16.9 %collective-permute-start.2 = (bf16[528,256]{1,0:T(8,128)(2,1)S(1)}, bf16[528,256]{1,0:T(8,128)(2,1)S(1)}, u32[]{:S(2)}, u32[]{:S(2)}) collective-permute-start(bf16[528,256]{1,0:T(8,128)(2,1)S(1)} %get-tuple-element.20), channel_id=1, source_target_pairs={{0,96},{32,64},{64,32},{96,0},{1,97},{33,65},{65,33},{97,1},{2,98}... | collective-permute-start | bytes 811016 | tf_op jit(solution)/shard_map/ppermute | solution.py:184
  45.0 33.2 %all-to-all-start.1 = ((bf16[256,4,256]{2,1,0:T(4,128)(2,1)}), bf16[256,4,256]{2,1,0:T(4,128)(2,1)S(1)}, u32[]{:S(2)}, u32[]{:S(2)}) async-start(bf16[256,4,256]{2,1,0:T(4,128)(2,1)} %get-tuple-element.27), calls=%async_computation.1 | async-start | bytes 1048576 | tf_op jit(solution)/shard_map/all_to_all | solution.py:230
  57.0 10.5 %collective-permute-start.3 = (bf16[512,256]{1,0:T(8,128)(2,1)S(1)}, bf16[512,256]{1,0:T(8,128)(2,1)S(1)}, u32[]{:S(2)}, u32[]{:S(2)}) collective-permute-start(bf16[512,256]{1,0:T(8,128)(2,1)S(1)} %get-tuple-element.22), channel_id=1, source_target_pairs={{0,32},{32,0},{64,96},{96,64},{1,33},{33,1},{65,97},{97,65},{2,34}... | collective-permute-start | bytes 786440 | tf_op jit(solution)/shard_map/ppermute | solution.py:184
  58.5 12.3 %collective-permute-start.4 = (bf16[512,256]{1,0:T(8,128)(2,1)S(1)}, bf16[512,256]{1,0:T(8,128)(2,1)S(1)}, u32[]{:S(2)}, u32[]{:S(2)}) collective-permute-start(bf16[512,256]{1,0:T(8,128)(2,1)S(1)} %get-tuple-element.23), channel_id=1, source_target_pairs={{0,64},{32,96},{64,0},{96,32},{1,65},{33,97},{65,1},{97,33},{2,66}... | collective-permute-start | bytes 786440 | tf_op jit(solution)/shard_map/ppermute | solution.py:184
  59.7 16.8 %collective-permute-start.5 = (bf16[512,256]{1,0:T(8,128)(2,1)S(1)}, bf16[512,256]{1,0:T(8,128)(2,1)S(1)}, u32[]{:S(2)}, u32[]{:S(2)}) collective-permute-start(bf16[512,256]{1,0:T(8,128)(2,1)S(1)} %get-tuple-element.24), channel_id=1, source_target_pairs={{0,96},{32,64},{64,32},{96,0},{1,97},{33,65},{65,33},{97,1},{2,98}... | collective-permute-start | bytes 786440 | tf_op jit(solution)/shard_map/ppermute | solution.py:184

commit v3 on v2

--- a/solution.py
+++ b/solution.py
@@ -18,6 +18,8 @@
 SIZES = {"h": HALVES, "g": GROUP, "z": ZSIZE, "tp": TP}
 AXES = tuple(SIZES)
 ORDER = ("h", "g", "z", "tp")
+MERGE = 10**11
+EARLY = (3,)
 UNPACK = 0
 EXTRA = 16
 
@@ -27,6 +29,7 @@
 PARAMS = pltpu.CompilerParams(vmem_limit_bytes=32 * 2**20)
 SMEM = pl.BlockSpec(memory_space=pltpu.SMEM)
 VMEM = pl.BlockSpec(memory_space=pltpu.VMEM)
+HBM = pl.BlockSpec(memory_space=pltpu.HBM)
 
 
 def stride(axis):
@@ -37,26 +40,63 @@
     return sum(i * stride(axis) for axis, i in at.items())
 
 
-def pack_kernel(place_ref, last_ref, q_ref, c_ref, *out_refs):
-    tok, width = q_ref.shape[0], out_refs[0].shape[1]
-    half = EXTRA // 2
+def columns_of(k, width):
+    return pl.ds(pl.multiple_of((lax.axis_index("g") ^ k) * width, width), width)
+
+
+def prepare_kernel(last_ref, k_ref, v_ref, q_ref, c_ref, kv_out, *refs):
+    outs, (last_s, k_s, v_s, last_sem, kv_sems, sems) = refs[:GROUP], refs[GROUP:]
+    tok, width = q_ref.shape[0], outs[0].shape[1]
+    small = [
+        pltpu.make_async_copy(k_ref, k_s, kv_sems.at[0]),
+        pltpu.make_async_copy(v_ref, v_s, kv_sems.at[1]),
+        pltpu.make_async_copy(last_ref, last_s, last_sem),
+    ]
+    large = []
+    for k, out in enumerate(outs):
+        cols = columns_of(k, width)
+        for i, ref in enumerate((q_ref, c_ref)):
+            rows = pl.ds(i * tok, tok)
+            large.append(pltpu.make_async_copy(ref.at[:, cols], out.at[rows, :], sems.at[2 * k + i]))
+    for copy in small + large:
+        copy.start()
+    small[0].wait()
+    small[1].wait()
+    for t in range(TP):
+        for g in range(GROUP):
+            col = (t * GROUP + g) * width
+            piece = jnp.concatenate([k_s[:, col : col + width], v_s[:, col : col + width]], axis=0)
+            for h in range(HALVES):
+                for z in range(ZSIZE):
+                    kv_out[source(h=h, g=g, z=z, tp=t)] = piece
+    small[2].wait()
     rows = lax.broadcasted_iota(jnp.int32, (EXTRA, width), 0)
-    frames = jnp.where(rows < half, last_ref[0], last_ref[1])
+    frames = jnp.where(rows < EXTRA // 2, last_s[0], last_s[1])
     frames = frames.astype(jnp.float32).astype(jnp.bfloat16)
-    for k, out in enumerate(out_refs):
-        cols = pl.ds(pl.multiple_of((place_ref[0] ^ k) * width, width), width)
-        out[0:tok, :] = q_ref[:, cols]
-        out[tok : 2 * tok, :] = c_ref[:, cols]
+    for out in outs:
         out[2 * tok : 2 * tok + EXTRA, :] = frames
-
-
-def unpack_kernel(place_ref, *refs):
-    block_refs, (att_ref, dq_ref) = refs[:GROUP], refs[GROUP:]
-    tok, width = att_ref.shape[0], block_refs[0].shape[1]
-    for k, block in enumerate(block_refs):
-        cols = pl.ds(pl.multiple_of((place_ref[0] ^ k) * width, width), width)
-        att_ref[:, cols] = block[0:tok, :]
-        dq_ref[:, cols] = block[tok : 2 * tok, :]
+    for copy in large:
+        copy.wait()
+
+
+def merge_kernel(*refs):
+    for j, ref in enumerate(refs[:-1]):
+        refs[-1][j] = ref[...]
+
+
+def unpack_kernel(*refs):
+    blocks, (att_ref, dq_ref, sems) = refs[:GROUP], refs[GROUP:]
+    tok, width = att_ref.shape[0], blocks[0].shape[1]
+    copies = []
+    for k, block in enumerate(blocks):
+        for i, out in enumerate((att_ref, dq_ref)):
+            rows = pl.ds(i * tok, tok)
+            cols = columns_of(k, width)
+            copies.append(pltpu.make_async_copy(block.at[rows, :], out.at[:, cols], sems.at[2 * k + i]))
+    for copy in copies:
+        copy.start()
+    for copy in copies:
+        copy.wait()
 
 
 def settle_kernel(in_ref, k_ref, v_ref):
@@ -77,9 +117,12 @@
     return lax.dot_general(a, b, (dims, ((), ())), preferred_element_type=jnp.float32)
 
 
-def attention_kernel(gate_ref, kv_ref, *refs):
-    msgs, outs = refs[:GROUP], refs[GROUP : 2 * GROUP]
-    grad_ref, k_s, v_s, dk_s, dv_s = refs[2 * GROUP :]
+def attention_kernel(gate_ref, kv_ref, early_ref, *refs):
+    late = GROUP - len(EARLY)
+    late_refs, outs = refs[:late], refs[late : late + GROUP]
+    grad_ref, k_s, v_s, dk_s, dv_s = refs[late + GROUP :]
+    msgs = {k: early_ref.at[i] for i, k in enumerate(EARLY)}
+    msgs |= zip((k for k in range(GROUP) if k not in EARLY), late_refs)
     tok = outs[0].shape[0] // 2
     lat, width = k_s.shape
     own = kv_ref.shape[1] // 2
@@ -90,14 +133,14 @@
     frame = place // stride("h") % HALVES * GROUP + place // stride("g") % GROUP
     frame = frame.astype(jnp.float32)
 
-    def bias(msg, i):
+    def bias(j, i):
         row = 2 * tok + i * (EXTRA // 2)
-        last = msg[row : row + 1, 0:DH].astype(jnp.float32)
+        last = msgs[j][row : row + 1, 0:DH].astype(jnp.float32)
         return jnp.where(frame <= jnp.concatenate([last] * (lat // DH), axis=1), 0.0, masked_fill)
 
     def step(first):
         blocks = range(first, first + BLOCKS)
-        biases = [bias(msgs[j], i) for j in blocks for i in range(tok // TBLK)]
+        biases = [bias(j, i) for j in blocks for i in range(tok // TBLK)]
         heads = []
         for h in range(width // DH):
             cols = slice(h * DH, (h + 1) * DH)
@@ -153,22 +196,11 @@
         grad_ref[:, i * own : (i + 1) * own, :] = piece
 
 
-def cut_kernel(k_ref, v_ref, out_ref):
-    width = out_ref.shape[2]
-    for t in range(TP):
-        for g in range(GROUP):
-            col = (t * GROUP + g) * width
-            piece = jnp.concatenate([k_ref[:, col : col + width], v_ref[:, col : col + width]], axis=0)
-            for h in range(HALVES):
-                for z in range(ZSIZE):
-                    out_ref[source(h=h, g=g, z=z, tp=t)] = piece
-
-
-def call(kernel, shapes, specs, *args, cost=0, **kwargs):
+def call(kernel, shapes, specs, *args, cost=0, out_spec=VMEM, **kwargs):
     if cost:
         kwargs["cost_estimate"] = pl.CostEstimate(flops=cost, bytes_accessed=0, transcendentals=0)
     name = kernel.__name__.removesuffix("_kernel")
-    out_specs = [VMEM] * len(shapes)
+    out_specs = [out_spec] * len(shapes)
     return pl.pallas_call(
         kernel,
         out_shape=shapes,
@@ -190,35 +222,49 @@
     width = columns // GROUP
     devices = HALVES * GROUP * ZSIZE * TP
     lat = own * devices
-    place = lax.axis_index("g").astype(jnp.int32).reshape(1)
     gate = jnp.tanh(gate_logit).astype(jnp.float32).reshape(1)
 
     def low(*shape):
         return jax.ShapeDtypeStruct(shape, jnp.bfloat16)
 
-    (both,) = call(
-        cut_kernel, [low(devices, 2 * own, width)], [VMEM] * 2, latent_keys, latent_values
-    )
-    both = lax.all_to_all(both, ORDER, 0, 0)
-
-    msgs = call(
-        pack_kernel,
-        [low(2 * tok + EXTRA, width)] * GROUP,
-        [SMEM, SMEM, VMEM, VMEM],
-        place,
+    kv_shape = low(devices, 2 * own, width)
+    last_frame, latent_keys, latent_values, queries, cotangent = (
+        pltpu.with_memory_space_constraint(x, pltpu.HBM)
+        for x in (last_frame, latent_keys, latent_values, queries, cotangent)
+    )
+    both, *msgs = call(
+        prepare_kernel,
+        [kv_shape] + [low(2 * tok + EXTRA, width)] * GROUP,
+        [HBM] * 5,
         last_frame,
+        latent_keys,
+        latent_values,
         queries,
         cotangent,
-    )
+        scratch_shapes=[
+            pltpu.SMEM((last_frame.shape[0],), jnp.int32),
+            pltpu.VMEM((own, wide), jnp.bfloat16),
+            pltpu.VMEM((own, wide), jnp.bfloat16),
+            pltpu.SemaphoreType.DMA,
+            pltpu.SemaphoreType.DMA((2,)),
+            pltpu.SemaphoreType.DMA((2 * GROUP,)),
+        ],
+    )
+    both = lax.all_to_all(both, ORDER, 0, 0)
     msgs = [swap(x, "g", GROUP, k) for k, x in enumerate(msgs)]
+    early = low(len(EARLY), 2 * tok + EXTRA, width)
+    early_msgs = [msgs[k] for k in EARLY]
+    (early,) = call(merge_kernel, [early], [VMEM] * len(EARLY), *early_msgs, cost=MERGE)
+    late_msgs = [x for k, x in enumerate(msgs) if k not in EARLY]
 
     *backs, terms = call(
         attention_kernel,
-        [low(2 * tok, width)] * GROUP + [low(devices, 2 * own, width)],
-        [SMEM] + [VMEM] * (1 + GROUP),
+        [low(2 * tok, width)] * GROUP + [kv_shape],
+        [SMEM] + [VMEM] * (2 + len(late_msgs)),
         gate,
         both,
-        *msgs,
+        early,
+        *late_msgs,
         scratch_shapes=[
             pltpu.VMEM((lat, width), jnp.bfloat16),
             pltpu.VMEM((lat, width), jnp.bfloat16),
@@ -233,7 +279,13 @@
 
     backs = [swap(x, "g", GROUP, k) for k, x in enumerate(backs)]
     attended, query_grad = call(
-        unpack_kernel, [low(tok, columns)] * 2, [SMEM] + [VMEM] * GROUP, place, *backs, cost=UNPACK
+        unpack_kernel,
+        [low(tok, columns)] * 2,
+        [VMEM] * GROUP,
+        *backs,
+        cost=UNPACK,
+        out_spec=HBM,
+        scratch_shapes=[pltpu.SemaphoreType.DMA((2 * GROUP,))],
     )
     return (attended, query_grad, key_grad, value_grad)
 

time: 79.3 us -> 74.2 us (0.936)
  starting transfers between devices: 33.2 us -> 28.5 us
  local copies, waits for them, and re-layouts: 2.07 us -> 0 us
  waiting for transfers between devices: 33.6 us -> 35 us
    all_to_all x1, waiting for transfers between devices: 0.28 us -> 9.13 us  [per_device(): both = lax.all_to_all(both, ORDER, 0, 0)]
    ppermute x6, waiting for transfers between devices: 32.8 us -> 25.3 us  [swap(): lax.ppermute(x, axis, [(i, i ^ k) for i in range(size)])]
    all_to_all x1, starting transfers between devices: 12.1 us -> 5.42 us  [per_device(): terms = lax.all_to_all(terms, ORDER, 0, 0)]
    ppermute x6, starting transfers between devices: 5.51 us -> 8.55 us  [swap(): lax.ppermute(x, axis, [(i, i ^ k) for i in range(size)])]
    unnamed x10 -> x0, local copies, waits for them, and re-layouts: 2.07 us -> none
    all_to_all x1, starting transfers between devices: 15.7 us -> 14.5 us  [per_device(): both = lax.all_to_all(both, ORDER, 0, 0)]
  transfers between devices with their start and end apart: 8 -> 8, of which waited for: 8 -> 7; matrix products, arithmetic and copies ran while one was open for 0% -> 0% of each run, Pallas kernels for 2% -> 1%
where the time goes in v3:
time: 74.2 us; the launch traced here: 74 us
  waiting for transfers between devices  35 us (47%)
  starting transfers between devices  28.5 us (38%)
  Pallas kernels  9.11 us (12%)
  between operations  1.38 us (2%)
    ppermute x6, waiting for transfers between devices, swap(): lax.ppermute(x, axis, [(i, i ^ k) for i in range(size)])  25.3 us
    all_to_all x1, starting transfers between devices, per_device(): both = lax.all_to_all(both, ORDER, 0, 0)  14.5 us
    all_to_all x1, waiting for transfers between devices, per_device(): both = lax.all_to_all(both, ORDER, 0, 0)  9.13 us
    pallas_call x5, Pallas kernels, call(): pl.pallas_call(kernel, out_shape=shapes, in_specs=specs, out_specs=out_sp...  9.11 us
    ppermute x6, starting transfers between devices, swap(): lax.ppermute(x, axis, [(i, i ^ k) for i in range(size)])  8.55 us
    all_to_all x1, starting transfers between devices, per_device(): terms = lax.all_to_all(terms, ORDER, 0, 0)  5.42 us
  transfers between devices with their start and end apart: 8, of which 7 were waited for; matrix products, arithmetic and copies ran while one was open for 0% of the time, Pallas kernels for 1%

profile of v3, /device:TPU:1, one launch (start us, length us, event | category | flops | bytes accessed | tf_op | source)
XLA Modules:
  0.0 74.0 jit_solution(11475703283448347794)
XLA Ops:
  0.6 2.2 %prepare.1 = (bf16[256,4,256]{2,1,0:T(4,128)(2,1)}, bf16[528,256]{1,0:T(8,128)(2,1)S(1)}, bf16[528,256]{1,0:T(8,128)(2,1)S(1)}, bf16[528,256]{1,0:T(8,128)(2,1)S(1)}, bf16[528,256]{1,0:T(8,128)(2,1)S(1)}) custom-call(s32[2]{0:T(128)} %last_ref.1, bf16[2,4096]{1,0:T(2,128)(2,1)} %k_ref.1, bf16[2,4096]{1,0:T(2,128)(2,1)} %v_ref.1, bf16[256,1024]{1,0:T(8,128)(2,1)} %q_ref.1, ...), custom_call_target="tpu_custom_call" | custom-call | tf_op jit(solution)/shard_map/prepare/pallas_call | solution.py:204
  2.9 3.1 %collective-permute-start = (bf16[528,256]{1,0:T(8,128)(2,1)S(1)}, bf16[528,256]{1,0:T(8,128)(2,1)S(1)}, u32[]{:S(2)}, u32[]{:S(2)}) collective-permute-start(bf16[528,256]{1,0:T(8,128)(2,1)S(1)} %get-tuple-element.19), channel_id=1, source_target_pairs={{0,96},{32,64},{64,32},{96,0},{1,97},{33,65},{65,33},{97,1},{2,98}... | collective-permute-start | bytes 811016 | tf_op jit(solution)/shard_map/ppermute | solution.py:216
  6.0 14.5 %all-to-all-start = ((bf16[256,4,256]{2,1,0:T(4,128)(2,1)}), bf16[256,4,256]{2,1,0:T(4,128)(2,1)S(1)}, u32[]{:S(2)}, u32[]{:S(2)}) async-start(bf16[256,4,256]{2,1,0:T(4,128)(2,1)} %get-tuple-element.18), calls=%async_computation | async-start | bytes 1048576 | tf_op jit(solution)/shard_map/all_to_all | solution.py:253
  20.5 1.5 %collective-permute-start.1 = (bf16[528,256]{1,0:T(8,128)(2,1)S(1)}, bf16[528,256]{1,0:T(8,128)(2,1)S(1)}, u32[]{:S(2)}, u32[]{:S(2)}) collective-permute-start(bf16[528,256]{1,0:T(8,128)(2,1)S(1)} %get-tuple-element.21), channel_id=1, source_target_pairs={{0,32},{32,0},{64,96},{96,64},{1,33},{33,1},{65,97},{97,65},{2,34}... | collective-permute-start | bytes 811016 | tf_op jit(solution)/shard_map/ppermute | solution.py:216
  22.0 1.2 %collective-permute-start.2 = (bf16[528,256]{1,0:T(8,128)(2,1)S(1)}, bf16[528,256]{1,0:T(8,128)(2,1)S(1)}, u32[]{:S(2)}, u32[]{:S(2)}) collective-permute-start(bf16[528,256]{1,0:T(8,128)(2,1)S(1)} %get-tuple-element.22), channel_id=1, source_target_pairs={{0,64},{32,96},{64,0},{96,32},{1,65},{33,97},{65,1},{97,33},{2,66}... | collective-permute-start | bytes 811016 | tf_op jit(solution)/shard_map/ppermute | solution.py:216
  23.9 0.0 collective-permute-done.refs_0_
  23.9 7.4 %collective-permute-done.1.refs_1_ = bf16[528,256]{1,0:T(8,128)(2,1)S(1)} collective-permute-done((bf16[528,256]{1,0:T(8,128)(2,1)S(1)}, bf16[528,256]{1,0:T(8,128)(2,1)S(1)}, u32[]{:S(2)}, u32[]{:S(2)}) %collective-permute-start.1) | collective-permute-done | bytes 270368 | tf_op jit(solution)/shard_map/ppermute | solution.py:216
  31.3 1.2 %collective-permute-done.2.refs_2_ = bf16[528,256]{1,0:T(8,128)(2,1)S(1)} collective-permute-done((bf16[528,256]{1,0:T(8,128)(2,1)S(1)}, bf16[528,256]{1,0:T(8,128)(2,1)S(1)}, u32[]{:S(2)}, u32[]{:S(2)}) %collective-permute-start.2) | collective-permute-done | bytes 270368 | tf_op jit(solution)/shard_map/ppermute | solution.py:216
  32.5 9.1 %all-to-all-done.kv_ref = bf16[256,4,256]{2,1,0:T(4,128)(2,1)S(1)} async-done(((bf16[256,4,256]{2,1,0:T(4,128)(2,1)}), bf16[256,4,256]{2,1,0:T(4,128)(2,1)S(1)}, u32[]{:S(2)}, u32[]{:S(2)}) %all-to-all-start) | async-done | bytes 524320 | tf_op jit(solution)/shard_map/all_to_all | solution.py:253
  41.6 5.1 %attention.1 = (bf16[512,256]{1,0:T(8,128)(2,1)S(1)}, bf16[512,256]{1,0:T(8,128)(2,1)S(1)}, bf16[512,256]{1,0:T(8,128)(2,1)S(1)}, bf16[512,256]{1,0:T(8,128)(2,1)S(1)}, bf16[256,4,256]{2,1,0:T(4,128)(2,1)}) custom-call(f32[1]{0:T(128)} %bitcast.gate_ref, bf16[256,4,256]{2,1,0:T(4,128)(2,1)S(1)} %all-to-all-done.kv_ref, ...), custom_call_target="tpu_custom_call" | custom-call | tf_op jit(solution)/shard_map/attention/pallas_call | solution.py:204
  46.7 5.4 %all-to-all-start.1 = ((bf16[256,4,256]{2,1,0:T(4,128)(2,1)}), bf16[256,4,256]{2,1,0:T(4,128)(2,1)S(1)}, u32[]{:S(2)}, u32[]{:S(2)}) async-start(bf16[256,4,256]{2,1,0:T(4,128)(2,1)} %get-tuple-element.29), calls=%async_computation.1 | async-start | bytes 1048576 | tf_op jit(solution)/shard_map/all_to_all | solution.py:276
  52.2 1.5 %collective-permute-start.3 = (bf16[512,256]{1,0:T(8,128)(2,1)S(1)}, bf16[512,256]{1,0:T(8,128)(2,1)S(1)}, u32[]{:S(2)}, u32[]{:S(2)}) collective-permute-start(bf16[512,256]{1,0:T(8,128)(2,1)S(1)} %get-tuple-element.24), channel_id=1, source_target_pairs={{0,32},{32,0},{64,96},{96,64},{1,33},{33,1},{65,97},{97,65},{2,34}... | collective-permute-start | bytes 786440 | tf_op jit(solution)/shard_map/ppermute | solution.py:216
  53.6 1.2 %collective-permute-start.4 = (bf16[512,256]{1,0:T(8,128)(2,1)S(1)}, bf16[512,256]{1,0:T(8,128)(2,1)S(1)}, u32[]{:S(2)}, u32[]{:S(2)}) collective-permute-start(bf16[512,256]{1,0:T(8,128)(2,1)S(1)} %get-tuple-element.25), channel_id=1, source_target_pairs={{0,64},{32,96},{64,0},{96,32},{1,65},{33,97},{65,1},{97,33},{2,66}... | collective-permute-start | bytes 786440 | tf_op jit(solution)/shard_map/ppermute | solution.py:216
  54.8 0.1 collective-permute-start.5
  54.9 7.7 %collective-permute-done.3.refs_1_ = bf16[512,256]{1,0:T(8,128)(2,1)S(1)} collective-permute-done((bf16[512,256]{1,0:T(8,128)(2,1)S(1)}, bf16[512,256]{1,0:T(8,128)(2,1)S(1)}, u32[]{:S(2)}, u32[]{:S(2)}) %collective-permute-start.3) | collective-permute-done | bytes 262176 | tf_op jit(solution)/shard_map/ppermute | solution.py:216
  62.6 3.3 %collective-permute-done.4.refs_2_ = bf16[512,256]{1,0:T(8,128)(2,1)S(1)} collective-permute-done((bf16[512,256]{1,0:T(8,128)(2,1)S(1)}, bf16[512,256]{1,0:T(8,128)(2,1)S(1)}, u32[]{:S(2)}, u32[]{:S(2)}) %collective-permute-start.4) | collective-permute-done | bytes 262176 | tf_op jit(solution)/shard_map/ppermute | solution.py:216
  66.0 5.7 %collective-permute-done.5.refs_3_ = bf16[512,256]{1,0:T(8,128)(2,1)S(1)} collective-permute-done((bf16[512,256]{1,0:T(8,128)(2,1)S(1)}, bf16[512,256]{1,0:T(8,128)(2,1)S(1)}, u32[]{:S(2)}, u32[]{:S(2)}) %collective-permute-start.5) | collective-permute-done | bytes 262176 | tf_op jit(solution)/shard_map/ppermute | solution.py:216
  71.6 1.0 %unpack.1 = (bf16[256,1024]{1,0:T(8,128)(2,1)}, bf16[256,1024]{1,0:T(8,128)(2,1)}) custom-call(bf16[512,256]{1,0:T(8,128)(2,1)S(1)} %get-tuple-element.23.refs_0_, bf16[512,256]{1,0:T(8,128)(2,1)S(1)} %collective-permute-done.3.refs_1_, bf16[512,256]{1,0:T(8,128)(2,1)S(1)} %collective-permute-done.4.refs_2_, bf16[512,256]{1,0:T(8,128)(2,1)S(1)} %collective-permute-done.5.refs_3_), custom_call_target="tpu_custom_call" | custom-call | tf_op jit(solution)/shard_map/unpack/pallas_call | solution.py:204
  72.7 0.6 all-to-all-done.1.in_ref
  73.3 0.7 settle.1
  (1 shorter events, 0.0 us)
Async XLA Ops:
  2.9 21.0 %collective-permute-start = (bf16[528,256]{1,0:T(8,128)(2,1)S(1)}, bf16[528,256]{1,0:T(8,128)(2,1)S(1)}, u32[]{:S(2)}, u32[]{:S(2)}) collective-permute-start(bf16[528,256]{1,0:T(8,128)(2,1)S(1)} %get-tuple-element.19), channel_id=1, source_target_pairs={{0,96},{32,64},{64,32},{96,0},{1,97},{33,65},{65,33},{97,1},{2,98}... | collective-permute-start | bytes 811016 | tf_op jit(solution)/shard_map/ppermute | solution.py:216
  6.0 35.6 %all-to-all-start = ((bf16[256,4,256]{2,1,0:T(4,128)(2,1)}), bf16[256,4,256]{2,1,0:T(4,128)(2,1)S(1)}, u32[]{:S(2)}, u32[]{:S(2)}) async-start(bf16[256,4,256]{2,1,0:T(4,128)(2,1)} %get-tuple-element.18), calls=%async_computation | async-start | bytes 1048576 | tf_op jit(solution)/shard_map/all_to_all | solution.py:253
  20.5 10.8 %collective-permute-start.1 = (bf16[528,256]{1,0:T(8,128)(2,1)S(1)}, bf16[528,256]{1,0:T(8,128)(2,1)S(1)}, u32[]{:S(2)}, u32[]{:S(2)}) collective-permute-start(bf16[528,256]{1,0:T(8,128)(2,1)S(1)} %get-tuple-element.21), channel_id=1, source_target_pairs={{0,32},{32,0},{64,96},{96,64},{1,33},{33,1},{65,97},{97,65},{2,34}... | collective-permute-start | bytes 811016 | tf_op jit(solution)/shard_map/ppermute | solution.py:216
  22.0 10.5 %collective-permute-start.2 = (bf16[528,256]{1,0:T(8,128)(2,1)S(1)}, bf16[528,256]{1,0:T(8,128)(2,1)S(1)}, u32[]{:S(2)}, u32[]{:S(2)}) collective-permute-start(bf16[528,256]{1,0:T(8,128)(2,1)S(1)} %get-tuple-element.22), channel_id=1, source_target_pairs={{0,64},{32,96},{64,0},{96,32},{1,65},{33,97},{65,1},{97,33},{2,66}... | collective-permute-start | bytes 811016 | tf_op jit(solution)/shard_map/ppermute | solution.py:216
  46.7 26.6 %all-to-all-start.1 = ((bf16[256,4,256]{2,1,0:T(4,128)(2,1)}), bf16[256,4,256]{2,1,0:T(4,128)(2,1)S(1)}, u32[]{:S(2)}, u32[]{:S(2)}) async-start(bf16[256,4,256]{2,1,0:T(4,128)(2,1)} %get-tuple-element.29), calls=%async_computation.1 | async-start | bytes 1048576 | tf_op jit(solution)/shard_map/all_to_all | solution.py:276
  52.2 10.5 %collective-permute-start.3 = (bf16[512,256]{1,0:T(8,128)(2,1)S(1)}, bf16[512,256]{1,0:T(8,128)(2,1)S(1)}, u32[]{:S(2)}, u32[]{:S(2)}) collective-permute-start(bf16[512,256]{1,0:T(8,128)(2,1)S(1)} %get-tuple-element.24), channel_id=1, source_target_pairs={{0,32},{32,0},{64,96},{96,64},{1,33},{33,1},{65,97},{97,65},{2,34}... | collective-permute-start | bytes 786440 | tf_op jit(solution)/shard_map/ppermute | solution.py:216
  53.6 12.3 %collective-permute-start.4 = (bf16[512,256]{1,0:T(8,128)(2,1)S(1)}, bf16[512,256]{1,0:T(8,128)(2,1)S(1)}, u32[]{:S(2)}, u32[]{:S(2)}) collective-permute-start(bf16[512,256]{1,0:T(8,128)(2,1)S(1)} %get-tuple-element.25), channel_id=1, source_target_pairs={{0,64},{32,96},{64,0},{96,32},{1,65},{33,97},{65,1},{97,33},{2,66}... | collective-permute-start | bytes 786440 | tf_op jit(solution)/shard_map/ppermute | solution.py:216
  54.8 16.8 %collective-permute-start.5 = (bf16[512,256]{1,0:T(8,128)(2,1)S(1)}, bf16[512,256]{1,0:T(8,128)(2,1)S(1)}, u32[]{:S(2)}, u32[]{:S(2)}) collective-permute-start(bf16[512,256]{1,0:T(8,128)(2,1)S(1)} %get-tuple-element.26), channel_id=1, source_target_pairs={{0,96},{32,64},{64,32},{96,0},{1,97},{33,65},{65,33},{97,1},{2,98}... | collective-permute-start | bytes 786440 | tf_op jit(solution)/shard_map/ppermute | solution.py:216

commit v4 on v3

--- a/solution.py
+++ b/solution.py
@@ -65,7 +65,7 @@
     for t in range(TP):
         for g in range(GROUP):
             col = (t * GROUP + g) * width
-            piece = jnp.concatenate([k_s[:, col : col + width], v_s[:, col : col + width]], axis=0)
+            piece = jnp.concatenate([k_s[:, col : col + width], v_s[:, col : col + width]], axis=1)
             for h in range(HALVES):
                 for z in range(ZSIZE):
                     kv_out[source(h=h, g=g, z=z, tp=t)] = piece
@@ -100,17 +100,16 @@
 
 
 def settle_kernel(in_ref, k_ref, v_ref):
-    own, wide = k_ref.shape
-    width = in_ref.shape[2]
+    width = in_ref.shape[2] // 2
     for g in range(GROUP):
         for t in range(TP):
-            total = jnp.zeros((2 * own, width), jnp.float32)
+            total = jnp.zeros(in_ref.shape[1:], jnp.float32)
             for h in range(HALVES):
                 for z in range(ZSIZE):
                     total += in_ref[source(h=h, g=g, z=z, tp=t)].astype(jnp.float32)
             col = (t * GROUP + g) * width
-            k_ref[:, col : col + width] = total[0:own]
-            v_ref[:, col : col + width] = total[own:]
+            k_ref[:, col : col + width] = total[:, 0:width]
+            v_ref[:, col : col + width] = total[:, width:]
 
 
 def dot(a, b, dims):
@@ -125,10 +124,10 @@
     msgs |= zip((k for k in range(GROUP) if k not in EARLY), late_refs)
     tok = outs[0].shape[0] // 2
     lat, width = k_s.shape
-    own = kv_ref.shape[1] // 2
+    own = kv_ref.shape[1]
     gate = gate_ref[0]
-    k_s[...] = kv_ref[:, 0:own, :].reshape(lat, width)
-    v_s[...] = kv_ref[:, own : 2 * own, :].reshape(lat, width)
+    k_s[...] = kv_ref[:, :, 0:width].reshape(lat, width)
+    v_s[...] = kv_ref[:, :, width:].reshape(lat, width)
     place = lax.broadcasted_iota(jnp.int32, (1, lat), 1) // own
     frame = place // stride("h") % HALVES * GROUP + place // stride("g") % GROUP
     frame = frame.astype(jnp.float32)
@@ -175,10 +174,10 @@
             out = (SCALE * dot(sgrad, keys, ((1,), (0,)))).astype(jnp.bfloat16)
             for i, j in enumerate(blocks):
                 outs[j][tok : 2 * tok, cols] = out[i * tok : (i + 1) * tok]
-            dk = dot(sgrad, q, ((0,), (0,)))
-            dv = dot(low, gcot, ((0,), (0,)))
-            dk_s[:, cols] = dk if first == 0 else dk_s[:, cols] + dk
-            dv_s[:, cols] = dv if first == 0 else dv_s[:, cols] + dv
+            dk = dot(q.T, sgrad, ((1,), (0,)))
+            dv = dot(gcot.T, low, ((1,), (0,)))
+            dk_s[cols, :] = dk if first == 0 else dk_s[cols, :] + dk
+            dv_s[cols, :] = dv if first == 0 else dv_s[cols, :] + dv
 
         one, two = heads
         weights1, grads1 = softmax(one), prob_grads(one)
@@ -192,8 +191,8 @@
     for first in range(0, GROUP, BLOCKS):
         step(first)
     for i, grads in enumerate((SCALE * dk_s[...], dv_s[...])):
-        piece = grads.astype(jnp.bfloat16).reshape(lat // own, own, width)
-        grad_ref[:, i * own : (i + 1) * own, :] = piece
+        piece = grads.T.astype(jnp.bfloat16).reshape(lat // own, own, width)
+        grad_ref[:, :, i * width : (i + 1) * width] = piece
 
 
 def call(kernel, shapes, specs, *args, cost=0, out_spec=VMEM, **kwargs):
@@ -227,7 +226,7 @@
     def low(*shape):
         return jax.ShapeDtypeStruct(shape, jnp.bfloat16)
 
-    kv_shape = low(devices, 2 * own, width)
+    kv_shape = low(devices, own, 2 * width)
     last_frame, latent_keys, latent_values, queries, cotangent = (
         pltpu.with_memory_space_constraint(x, pltpu.HBM)
         for x in (last_frame, latent_keys, latent_values, queries, cotangent)
@@ -268,8 +267,8 @@
         scratch_shapes=[
             pltpu.VMEM((lat, width), jnp.bfloat16),
             pltpu.VMEM((lat, width), jnp.bfloat16),
-            pltpu.VMEM((lat, width), jnp.float32),
-            pltpu.VMEM((lat, width), jnp.float32),
+            pltpu.VMEM((width, lat), jnp.float32),
+            pltpu.VMEM((width, lat), jnp.float32),
         ],
     )
 

time: 74.2 us -> 73.8 us (level)
  no operation moved by 1% of the time
where the time goes in v4:
time: 73.8 us; the launch traced here: 73.6 us
  waiting for transfers between devices  35 us (47%)
  starting transfers between devices  28.5 us (39%)
  Pallas kernels  8.63 us (12%)
  between operations  1.38 us (2%)
    ppermute x6, waiting for transfers between devices, swap(): lax.ppermute(x, axis, [(i, i ^ k) for i in range(size)])  25.3 us
    all_to_all x1, starting transfers between devices, per_device(): both = lax.all_to_all(both, ORDER, 0, 0)  14.5 us
    all_to_all x1, waiting for transfers between devices, per_device(): both = lax.all_to_all(both, ORDER, 0, 0)  9.13 us
    pallas_call x5, Pallas kernels, call(): pl.pallas_call(kernel, out_shape=shapes, in_specs=specs, out_specs=out_sp...  8.63 us
    ppermute x6, starting transfers between devices, swap(): lax.ppermute(x, axis, [(i, i ^ k) for i in range(size)])  8.55 us
    all_to_all x1, starting transfers between devices, per_device(): terms = lax.all_to_all(terms, ORDER, 0, 0)  5.42 us
  transfers between devices with their start and end apart: 8, of which 7 were waited for; matrix products, arithmetic and copies ran while one was open for 0% of the time, Pallas kernels for 1%

profile of v4, /device:TPU:1, one launch (start us, length us, event | category | flops | bytes accessed | tf_op | source)
XLA Modules:
  0.0 73.6 jit_solution(8951785865075423202)
XLA Ops:
  0.6 2.2 %prepare.1 = (bf16[256,2,512]{2,1,0:T(2,128)(2,1)}, bf16[528,256]{1,0:T(8,128)(2,1)S(1)}, bf16[528,256]{1,0:T(8,128)(2,1)S(1)}, bf16[528,256]{1,0:T(8,128)(2,1)S(1)}, bf16[528,256]{1,0:T(8,128)(2,1)S(1)}) custom-call(s32[2]{0:T(128)} %last_ref.1, bf16[2,4096]{1,0:T(2,128)(2,1)} %k_ref.1, bf16[2,4096]{1,0:T(2,128)(2,1)} %v_ref.1, bf16[256,1024]{1,0:T(8,128)(2,1)} %q_ref.1, ...), custom_call_target="tpu_custom_call" | custom-call | tf_op jit(solution)/shard_map/prepare/pallas_call | solution.py:203
  2.9 3.1 %collective-permute-start = (bf16[528,256]{1,0:T(8,128)(2,1)S(1)}, bf16[528,256]{1,0:T(8,128)(2,1)S(1)}, u32[]{:S(2)}, u32[]{:S(2)}) collective-permute-start(bf16[528,256]{1,0:T(8,128)(2,1)S(1)} %get-tuple-element.19), channel_id=1, source_target_pairs={{0,96},{32,64},{64,32},{96,0},{1,97},{33,65},{65,33},{97,1},{2,98}... | collective-permute-start | bytes 811016 | tf_op jit(solution)/shard_map/ppermute | solution.py:215
  6.0 14.5 %all-to-all-start = ((bf16[256,2,512]{2,1,0:T(2,128)(2,1)}), bf16[256,2,512]{2,1,0:T(2,128)(2,1)S(1)}, u32[]{:S(2)}, u32[]{:S(2)}) async-start(bf16[256,2,512]{2,1,0:T(2,128)(2,1)} %get-tuple-element.18), calls=%async_computation | async-start | bytes 1048576 | tf_op jit(solution)/shard_map/all_to_all | solution.py:252
  20.5 1.5 %collective-permute-start.1 = (bf16[528,256]{1,0:T(8,128)(2,1)S(1)}, bf16[528,256]{1,0:T(8,128)(2,1)S(1)}, u32[]{:S(2)}, u32[]{:S(2)}) collective-permute-start(bf16[528,256]{1,0:T(8,128)(2,1)S(1)} %get-tuple-element.21), channel_id=1, source_target_pairs={{0,32},{32,0},{64,96},{96,64},{1,33},{33,1},{65,97},{97,65},{2,34}... | collective-permute-start | bytes 811016 | tf_op jit(solution)/shard_map/ppermute | solution.py:215
  22.0 1.2 %collective-permute-start.2 = (bf16[528,256]{1,0:T(8,128)(2,1)S(1)}, bf16[528,256]{1,0:T(8,128)(2,1)S(1)}, u32[]{:S(2)}, u32[]{:S(2)}) collective-permute-start(bf16[528,256]{1,0:T(8,128)(2,1)S(1)} %get-tuple-element.22), channel_id=1, source_target_pairs={{0,64},{32,96},{64,0},{96,32},{1,65},{33,97},{65,1},{97,33},{2,66}... | collective-permute-start | bytes 811016 | tf_op jit(solution)/shard_map/ppermute | solution.py:215
  23.9 0.0 collective-permute-done.refs_0_
  23.9 7.4 %collective-permute-done.1.refs_1_ = bf16[528,256]{1,0:T(8,128)(2,1)S(1)} collective-permute-done((bf16[528,256]{1,0:T(8,128)(2,1)S(1)}, bf16[528,256]{1,0:T(8,128)(2,1)S(1)}, u32[]{:S(2)}, u32[]{:S(2)}) %collective-permute-start.1) | collective-permute-done | bytes 270368 | tf_op jit(solution)/shard_map/ppermute | solution.py:215
  31.3 1.2 %collective-permute-done.2.refs_2_ = bf16[528,256]{1,0:T(8,128)(2,1)S(1)} collective-permute-done((bf16[528,256]{1,0:T(8,128)(2,1)S(1)}, bf16[528,256]{1,0:T(8,128)(2,1)S(1)}, u32[]{:S(2)}, u32[]{:S(2)}) %collective-permute-start.2) | collective-permute-done | bytes 270368 | tf_op jit(solution)/shard_map/ppermute | solution.py:215
  32.5 9.1 %all-to-all-done.kv_ref = bf16[256,2,512]{2,1,0:T(2,128)(2,1)S(1)} async-done(((bf16[256,2,512]{2,1,0:T(2,128)(2,1)}), bf16[256,2,512]{2,1,0:T(2,128)(2,1)S(1)}, u32[]{:S(2)}, u32[]{:S(2)}) %all-to-all-start) | async-done | bytes 524320 | tf_op jit(solution)/shard_map/all_to_all | solution.py:252
  41.6 4.7 %attention.1 = (bf16[512,256]{1,0:T(8,128)(2,1)S(1)}, bf16[512,256]{1,0:T(8,128)(2,1)S(1)}, bf16[512,256]{1,0:T(8,128)(2,1)S(1)}, bf16[512,256]{1,0:T(8,128)(2,1)S(1)}, bf16[256,2,512]{2,1,0:T(2,128)(2,1)}) custom-call(f32[1]{0:T(128)} %bitcast.gate_ref, bf16[256,2,512]{2,1,0:T(2,128)(2,1)S(1)} %all-to-all-done.kv_ref, ...), custom_call_target="tpu_custom_call" | custom-call | tf_op jit(solution)/shard_map/attention/pallas_call | solution.py:203
  46.3 5.4 %all-to-all-start.1 = ((bf16[256,2,512]{2,1,0:T(2,128)(2,1)}), bf16[256,2,512]{2,1,0:T(2,128)(2,1)S(1)}, u32[]{:S(2)}, u32[]{:S(2)}) async-start(bf16[256,2,512]{2,1,0:T(2,128)(2,1)} %get-tuple-element.29), calls=%async_computation.1 | async-start | bytes 1048576 | tf_op jit(solution)/shard_map/all_to_all | solution.py:275
  51.7 1.5 %collective-permute-start.3 = (bf16[512,256]{1,0:T(8,128)(2,1)S(1)}, bf16[512,256]{1,0:T(8,128)(2,1)S(1)}, u32[]{:S(2)}, u32[]{:S(2)}) collective-permute-start(bf16[512,256]{1,0:T(8,128)(2,1)S(1)} %get-tuple-element.24), channel_id=1, source_target_pairs={{0,32},{32,0},{64,96},{96,64},{1,33},{33,1},{65,97},{97,65},{2,34}... | collective-permute-start | bytes 786440 | tf_op jit(solution)/shard_map/ppermute | solution.py:215
  53.2 1.2 %collective-permute-start.4 = (bf16[512,256]{1,0:T(8,128)(2,1)S(1)}, bf16[512,256]{1,0:T(8,128)(2,1)S(1)}, u32[]{:S(2)}, u32[]{:S(2)}) collective-permute-start(bf16[512,256]{1,0:T(8,128)(2,1)S(1)} %get-tuple-element.25), channel_id=1, source_target_pairs={{0,64},{32,96},{64,0},{96,32},{1,65},{33,97},{65,1},{97,33},{2,66}... | collective-permute-start | bytes 786440 | tf_op jit(solution)/shard_map/ppermute | solution.py:215
  54.4 0.1 collective-permute-start.5
  54.5 7.7 %collective-permute-done.3.refs_1_ = bf16[512,256]{1,0:T(8,128)(2,1)S(1)} collective-permute-done((bf16[512,256]{1,0:T(8,128)(2,1)S(1)}, bf16[512,256]{1,0:T(8,128)(2,1)S(1)}, u32[]{:S(2)}, u32[]{:S(2)}) %collective-permute-start.3) | collective-permute-done | bytes 262176 | tf_op jit(solution)/shard_map/ppermute | solution.py:215
  62.2 3.3 %collective-permute-done.4.refs_2_ = bf16[512,256]{1,0:T(8,128)(2,1)S(1)} collective-permute-done((bf16[512,256]{1,0:T(8,128)(2,1)S(1)}, bf16[512,256]{1,0:T(8,128)(2,1)S(1)}, u32[]{:S(2)}, u32[]{:S(2)}) %collective-permute-start.4) | collective-permute-done | bytes 262176 | tf_op jit(solution)/shard_map/ppermute | solution.py:215
  65.5 5.7 %collective-permute-done.5.refs_3_ = bf16[512,256]{1,0:T(8,128)(2,1)S(1)} collective-permute-done((bf16[512,256]{1,0:T(8,128)(2,1)S(1)}, bf16[512,256]{1,0:T(8,128)(2,1)S(1)}, u32[]{:S(2)}, u32[]{:S(2)}) %collective-permute-start.5) | collective-permute-done | bytes 262176 | tf_op jit(solution)/shard_map/ppermute | solution.py:215
  71.2 1.0 %unpack.1 = (bf16[256,1024]{1,0:T(8,128)(2,1)}, bf16[256,1024]{1,0:T(8,128)(2,1)}) custom-call(bf16[512,256]{1,0:T(8,128)(2,1)S(1)} %get-tuple-element.23.refs_0_, bf16[512,256]{1,0:T(8,128)(2,1)S(1)} %collective-permute-done.3.refs_1_, bf16[512,256]{1,0:T(8,128)(2,1)S(1)} %collective-permute-done.4.refs_2_, bf16[512,256]{1,0:T(8,128)(2,1)S(1)} %collective-permute-done.5.refs_3_), custom_call_target="tpu_custom_call" | custom-call | tf_op jit(solution)/shard_map/unpack/pallas_call | solution.py:203
  72.2 0.6 all-to-all-done.1.in_ref
  72.9 0.7 settle.1
  (1 shorter events, 0.0 us)
Async XLA Ops:
  2.9 21.0 %collective-permute-start = (bf16[528,256]{1,0:T(8,128)(2,1)S(1)}, bf16[528,256]{1,0:T(8,128)(2,1)S(1)}, u32[]{:S(2)}, u32[]{:S(2)}) collective-permute-start(bf16[528,256]{1,0:T(8,128)(2,1)S(1)} %get-tuple-element.19), channel_id=1, source_target_pairs={{0,96},{32,64},{64,32},{96,0},{1,97},{33,65},{65,33},{97,1},{2,98}... | collective-permute-start | bytes 811016 | tf_op jit(solution)/shard_map/ppermute | solution.py:215
  6.0 35.6 %all-to-all-start = ((bf16[256,2,512]{2,1,0:T(2,128)(2,1)}), bf16[256,2,512]{2,1,0:T(2,128)(2,1)S(1)}, u32[]{:S(2)}, u32[]{:S(2)}) async-start(bf16[256,2,512]{2,1,0:T(2,128)(2,1)} %get-tuple-element.18), calls=%async_computation | async-start | bytes 1048576 | tf_op jit(solution)/shard_map/all_to_all | solution.py:252
  20.5 10.8 %collective-permute-start.1 = (bf16[528,256]{1,0:T(8,128)(2,1)S(1)}, bf16[528,256]{1,0:T(8,128)(2,1)S(1)}, u32[]{:S(2)}, u32[]{:S(2)}) collective-permute-start(bf16[528,256]{1,0:T(8,128)(2,1)S(1)} %get-tuple-element.21), channel_id=1, source_target_pairs={{0,32},{32,0},{64,96},{96,64},{1,33},{33,1},{65,97},{97,65},{2,34}... | collective-permute-start | bytes 811016 | tf_op jit(solution)/shard_map/ppermute | solution.py:215
  22.0 10.5 %collective-permute-start.2 = (bf16[528,256]{1,0:T(8,128)(2,1)S(1)}, bf16[528,256]{1,0:T(8,128)(2,1)S(1)}, u32[]{:S(2)}, u32[]{:S(2)}) collective-permute-start(bf16[528,256]{1,0:T(8,128)(2,1)S(1)} %get-tuple-element.22), channel_id=1, source_target_pairs={{0,64},{32,96},{64,0},{96,32},{1,65},{33,97},{65,1},{97,33},{2,66}... | collective-permute-start | bytes 811016 | tf_op jit(solution)/shard_map/ppermute | solution.py:215
  46.3 26.6 %all-to-all-start.1 = ((bf16[256,2,512]{2,1,0:T(2,128)(2,1)}), bf16[256,2,512]{2,1,0:T(2,128)(2,1)S(1)}, u32[]{:S(2)}, u32[]{:S(2)}) async-start(bf16[256,2,512]{2,1,0:T(2,128)(2,1)} %get-tuple-element.29), calls=%async_computation.1 | async-start | bytes 1048576 | tf_op jit(solution)/shard_map/all_to_all | solution.py:275
  51.7 10.5 %collective-permute-start.3 = (bf16[512,256]{1,0:T(8,128)(2,1)S(1)}, bf16[512,256]{1,0:T(8,128)(2,1)S(1)}, u32[]{:S(2)}, u32[]{:S(2)}) collective-permute-start(bf16[512,256]{1,0:T(8,128)(2,1)S(1)} %get-tuple-element.24), channel_id=1, source_target_pairs={{0,32},{32,0},{64,96},{96,64},{1,33},{33,1},{65,97},{97,65},{2,34}... | collective-permute-start | bytes 786440 | tf_op jit(solution)/shard_map/ppermute | solution.py:215
  53.2 12.3 %collective-permute-start.4 = (bf16[512,256]{1,0:T(8,128)(2,1)S(1)}, bf16[512,256]{1,0:T(8,128)(2,1)S(1)}, u32[]{:S(2)}, u32[]{:S(2)}) collective-permute-start(bf16[512,256]{1,0:T(8,128)(2,1)S(1)} %get-tuple-element.25), channel_id=1, source_target_pairs={{0,64},{32,96},{64,0},{96,32},{1,65},{33,97},{65,1},{97,33},{2,66}... | collective-permute-start | bytes 786440 | tf_op jit(solution)/shard_map/ppermute | solution.py:215
  54.4 16.8 %collective-permute-start.5 = (bf16[512,256]{1,0:T(8,128)(2,1)S(1)}, bf16[512,256]{1,0:T(8,128)(2,1)S(1)}, u32[]{:S(2)}, u32[]{:S(2)}) collective-permute-start(bf16[512,256]{1,0:T(8,128)(2,1)S(1)} %get-tuple-element.26), channel_id=1, source_target_pairs={{0,96},{32,64},{64,32},{96,0},{1,97},{33,65},{65,33},{97,1},{2,98}... | collective-permute-start | bytes 786440 | tf_op jit(solution)/shard_map/ppermute | solution.py:215

commit v5 on v4

--- a/solution.py
+++ b/solution.py
@@ -11,15 +11,16 @@
 DH = 128
 TBLK = 128
 BLOCKS = 2
-GROUP = 4
-HALVES = 2
+GROUP = 8
+HALVES = 1
 ZSIZE = 8
 TP = 4
 SIZES = {"h": HALVES, "g": GROUP, "z": ZSIZE, "tp": TP}
 AXES = tuple(SIZES)
 ORDER = ("h", "g", "z", "tp")
 MERGE = 10**11
-EARLY = (3,)
+EARLY = (4, 5, 7)
+BACK_EARLY = (4, 5, 7)
 UNPACK = 0
 EXTRA = 16
 
@@ -137,49 +138,48 @@
         last = msgs[j][row : row + 1, 0:DH].astype(jnp.float32)
         return jnp.where(frame <= jnp.concatenate([last] * (lat // DH), axis=1), 0.0, masked_fill)
 
-    def step(first):
+    def load(first, h):
         blocks = range(first, first + BLOCKS)
+        cols = slice(h * DH, (h + 1) * DH)
+        q = jnp.concatenate([msgs[j][0:tok, cols] for j in blocks], axis=0)
+        cot = jnp.concatenate([msgs[j][tok : 2 * tok, cols] for j in blocks], axis=0)
+        gcot = (gate * cot.astype(jnp.float32)).astype(jnp.bfloat16)
+        return blocks, cols, q, gcot, k_s[:, cols], v_s[:, cols]
+
+    def softmax(chain):
+        blocks, _, q, _, keys, _ = chain
+        scores = dot(q, keys, ((1,), (1,)))
         biases = [bias(j, i) for j in blocks for i in range(tok // TBLK)]
-        heads = []
-        for h in range(width // DH):
-            cols = slice(h * DH, (h + 1) * DH)
-            q = jnp.concatenate([msgs[j][0:tok, cols] for j in blocks], axis=0)
-            cot = jnp.concatenate([msgs[j][tok : 2 * tok, cols] for j in blocks], axis=0)
-            gcot = (gate * cot.astype(jnp.float32)).astype(jnp.bfloat16)
-            heads.append((cols, q, gcot, k_s[:, cols], v_s[:, cols]))
-
-        def softmax(head):
-            _, q, _, keys, _ = head
-            scores = dot(q, keys, ((1,), (1,)))
-            parts = [
-                scores[i * TBLK : (i + 1) * TBLK] * (SCALE * LOG2E) + b for i, b in enumerate(biases)
-            ]
-            scores = jnp.concatenate(parts, axis=0)
-            expo = jnp.exp2(scores - jnp.max(scores, axis=-1, keepdims=True))
-            return expo * (1.0 / jnp.sum(expo, axis=-1, keepdims=True))
-
-        def prob_grads(head):
-            _, _, gcot, _, values = head
-            return dot(gcot, values, ((1,), (1,)))
-
-        def score_grads(weights, grads):
-            inner = jnp.sum(weights * grads, axis=-1, keepdims=True)
-            return (weights * (grads - inner)).astype(jnp.bfloat16)
-
-        def finish(head, low, sgrad):
-            cols, q, gcot, keys, values = head
-            out = (gate * dot(low, values, ((1,), (0,)))).astype(jnp.bfloat16)
-            for i, j in enumerate(blocks):
-                outs[j][0:tok, cols] = out[i * tok : (i + 1) * tok]
-            out = (SCALE * dot(sgrad, keys, ((1,), (0,)))).astype(jnp.bfloat16)
-            for i, j in enumerate(blocks):
-                outs[j][tok : 2 * tok, cols] = out[i * tok : (i + 1) * tok]
-            dk = dot(q.T, sgrad, ((1,), (0,)))
-            dv = dot(gcot.T, low, ((1,), (0,)))
-            dk_s[cols, :] = dk if first == 0 else dk_s[cols, :] + dk
-            dv_s[cols, :] = dv if first == 0 else dv_s[cols, :] + dv
-
-        one, two = heads
+        parts = [
+            scores[i * TBLK : (i + 1) * TBLK] * (SCALE * LOG2E) + b for i, b in enumerate(biases)
+        ]
+        scores = jnp.concatenate(parts, axis=0)
+        expo = jnp.exp2(scores - jnp.max(scores, axis=-1, keepdims=True))
+        return expo * (1.0 / jnp.sum(expo, axis=-1, keepdims=True))
+
+    def prob_grads(chain):
+        return dot(chain[3], chain[5], ((1,), (1,)))
+
+    def score_grads(weights, grads):
+        inner = jnp.sum(weights * grads, axis=-1, keepdims=True)
+        return (weights * (grads - inner)).astype(jnp.bfloat16)
+
+    def finish(chain, low, sgrad):
+        blocks, cols, q, gcot, keys, values = chain
+        out = (gate * dot(low, values, ((1,), (0,)))).astype(jnp.bfloat16)
+        for i, j in enumerate(blocks):
+            outs[j][0:tok, cols] = out[i * tok : (i + 1) * tok]
+        out = (SCALE * dot(sgrad, keys, ((1,), (0,)))).astype(jnp.bfloat16)
+        for i, j in enumerate(blocks):
+            outs[j][tok : 2 * tok, cols] = out[i * tok : (i + 1) * tok]
+        dk = dot(q.T, sgrad, ((1,), (0,)))
+        dv = dot(gcot.T, low, ((1,), (0,)))
+        dk_s[cols, :] = dk if blocks[0] == 0 else dk_s[cols, :] + dk
+        dv_s[cols, :] = dv if blocks[0] == 0 else dv_s[cols, :] + dv
+
+    chains = [(j, h) for j in range(0, GROUP, BLOCKS) for h in range(width // DH)]
+    for i in range(0, len(chains), 2):
+        one, two = load(*chains[i]), load(*chains[i + 1])
         weights1, grads1 = softmax(one), prob_grads(one)
         weights2 = softmax(two)
         low1, sgrad1 = weights1.astype(jnp.bfloat16), score_grads(weights1, grads1)
@@ -187,9 +187,6 @@
         finish(one, low1, sgrad1)
         low2, sgrad2 = weights2.astype(jnp.bfloat16), score_grads(weights2, grads2)
         finish(two, low2, sgrad2)
-
-    for first in range(0, GROUP, BLOCKS):
-        step(first)
     for i, grads in enumerate((SCALE * dk_s[...], dv_s[...])):
         piece = grads.T.astype(jnp.bfloat16).reshape(lat // own, own, width)
         grad_ref[:, :, i * width : (i + 1) * width] = piece
@@ -277,6 +274,12 @@
     key_grad, value_grad = call(settle_kernel, [grad] * 2, [VMEM], terms)
 
     backs = [swap(x, "g", GROUP, k) for k, x in enumerate(backs)]
+    if BACK_EARLY:
+        shape = low(len(BACK_EARLY), 2 * tok, width)
+        some = [backs[k] for k in BACK_EARLY]
+        (some,) = call(merge_kernel, [shape], [VMEM] * len(some), *some, cost=MERGE)
+        for i, k in enumerate(BACK_EARLY):
+            backs[k] = some[i]
     attended, query_grad = call(
         unpack_kernel,
         [low(tok, columns)] * 2,

time: 73.8 us -> 73.7 us (level)
  waiting for transfers between devices: 35 us -> 18.3 us
  starting transfers between devices: 28.5 us -> 45 us
    ppermute x6 -> x14, waiting for transfers between devices: 25.3 us -> 10.6 us  [swap(): lax.ppermute(x, axis, [(i, i ^ k) for i in range(size)])]
    ppermute x6 -> x14, starting transfers between devices: 8.55 us -> 23.1 us  [swap(): lax.ppermute(x, axis, [(i, i ^ k) for i in range(size)])]
    all_to_all x1, waiting for transfers between devices: 9.13 us -> 4.28 us  [per_device(): both = lax.all_to_all(both, ORDER, 0, 0)]
    all_to_all x1, starting transfers between devices: 5.42 us -> 8.85 us  [per_device(): terms = lax.all_to_all(terms, ORDER, 0, 0)]
    all_to_all x1, waiting for transfers between devices: 0.65 us -> 3.44 us  [per_device(): terms = lax.all_to_all(terms, ORDER, 0, 0)]
    all_to_all x1, starting transfers between devices: 14.5 us -> 13.1 us  [per_device(): both = lax.all_to_all(both, ORDER, 0, 0)]
    pallas_call x5 -> x6, Pallas kernels: 8.63 us -> 8.61 us  [call(): pl.pallas_call(kernel, out_shape=shapes, in_specs=specs, out_specs=out_sp...]
  transfers between devices with their start and end apart: 8 -> 16, of which waited for: 7 -> 6; matrix products, arithmetic and copies ran while one was open for 0% -> 0% of each run, Pallas kernels for 1% -> 2%
where the time goes in v5:
time: 73.7 us; the launch traced here: 73.4 us
  starting transfers between devices  45 us (61%)
  waiting for transfers between devices  18.3 us (25%)
  Pallas kernels  8.61 us (12%)
  between operations  1.41 us (2%)
    ppermute x14, starting transfers between devices, swap(): lax.ppermute(x, axis, [(i, i ^ k) for i in range(size)])  23.1 us
    all_to_all x1, starting transfers between devices, per_device(): both = lax.all_to_all(both, ORDER, 0, 0)  13.1 us
    ppermute x14, waiting for transfers between devices, swap(): lax.ppermute(x, axis, [(i, i ^ k) for i in range(size)])  10.6 us
    all_to_all x1, starting transfers between devices, per_device(): terms = lax.all_to_all(terms, ORDER, 0, 0)  8.85 us
    pallas_call x6, Pallas kernels, call(): pl.pallas_call(kernel, out_shape=shapes, in_specs=specs, out_specs=out_sp...  8.61 us
    all_to_all x1, waiting for transfers between devices, per_device(): both = lax.all_to_all(both, ORDER, 0, 0)  4.28 us
    all_to_all x1, waiting for transfers between devices, per_device(): terms = lax.all_to_all(terms, ORDER, 0, 0)  3.44 us
  transfers between devices with their start and end apart: 16, of which 6 were waited for; matrix products, arithmetic and copies ran while one was open for 0% of the time, Pallas kernels for 2%

profile of v5, /device:TPU:1, one launch (start us, length us, event | category | flops | bytes accessed | tf_op | source)
XLA Modules:
  0.0 73.4 jit_solution(14991654989219129835)
XLA Ops:
  0.6 2.2 %prepare.1 = (bf16[256,2,256]{2,1,0:T(2,128)(2,1)}, bf16[528,128]{1,0:T(8,128)(2,1)S(1)}, bf16[528,128]{1,0:T(8,128)(2,1)S(1)}, bf16[528,128]{1,0:T(8,128)(2,1)S...) custom-call(s32[2]{0:T(128)} %last_ref.1, ...), custom_call_target="tpu_custom_call" | custom-call | tf_op jit(solution)/shard_map/prepare/pallas_call | solution.py:200
  2.9 3.8 %collective-permute-start = (bf16[528,128]{1,0:T(8,128)(2,1)S(1)}, bf16[528,128]{1,0:T(8,128)(2,1)S(1)}, u32[]{:S(2)}, u32[]{:S(2)}) collective-permute-start(bf16[528,128]{1,0:T(8,128)(2,1)S(1)} %get-tuple-element.27), channel_id=1, source_target_pairs={{0,128},{32,160},{64,192},{96,224},{128,0},{160,32},{192,64},{224,... | collective-permute-start | bytes 405512 | tf_op jit(solution)/shard_map/ppermute | solution.py:212
  6.7 1.0 %collective-permute-start.1 = (bf16[528,128]{1,0:T(8,128)(2,1)S(1)}, bf16[528,128]{1,0:T(8,128)(2,1)S(1)}, u32[]{:S(2)}, u32[]{:S(2)}) collective-permute-start(bf16[528,128]{1,0:T(8,128)(2,1)S(1)} %get-tuple-element.28), channel_id=1, source_target_pairs={{0,160},{32,128},{64,224},{96,192},{128,32},{160,0},{192,96},{224,... | collective-permute-start | bytes 405512 | tf_op jit(solution)/shard_map/ppermute | solution.py:212
  7.7 2.7 %collective-permute-start.2 = (bf16[528,128]{1,0:T(8,128)(2,1)S(1)}, bf16[528,128]{1,0:T(8,128)(2,1)S(1)}, u32[]{:S(2)}, u32[]{:S(2)}) collective-permute-start(bf16[528,128]{1,0:T(8,128)(2,1)S(1)} %get-tuple-element.29), channel_id=1, source_target_pairs={{0,224},{32,192},{64,160},{96,128},{128,96},{160,64},{192,32},{224... | collective-permute-start | bytes 405512 | tf_op jit(solution)/shard_map/ppermute | solution.py:212
  10.4 13.1 %all-to-all-start = ((bf16[256,2,256]{2,1,0:T(2,128)(2,1)}), bf16[256,2,256]{2,1,0:T(2,128)(2,1)S(1)}, u32[]{:S(2)}, u32[]{:S(2)}) async-start(bf16[256,2,256]{2,1,0:T(2,128)(2,1)} %get-tuple-element.26), calls=%async_computation | async-start | bytes 524288 | tf_op jit(solution)/shard_map/all_to_all | solution.py:249
  23.5 1.5 %collective-permute-start.3 = (bf16[528,128]{1,0:T(8,128)(2,1)S(1)}, bf16[528,128]{1,0:T(8,128)(2,1)S(1)}, u32[]{:S(2)}, u32[]{:S(2)}) collective-permute-start(bf16[528,128]{1,0:T(8,128)(2,1)S(1)} %get-tuple-element.31), channel_id=1, source_target_pairs={{0,32},{32,0},{64,96},{96,64},{128,160},{160,128},{192,224},{224,1... | collective-permute-start | bytes 405512 | tf_op jit(solution)/shard_map/ppermute | solution.py:212
  25.0 1.2 %collective-permute-start.4 = (bf16[528,128]{1,0:T(8,128)(2,1)S(1)}, bf16[528,128]{1,0:T(8,128)(2,1)S(1)}, u32[]{:S(2)}, u32[]{:S(2)}) collective-permute-start(bf16[528,128]{1,0:T(8,128)(2,1)S(1)} %get-tuple-element.32), channel_id=1, source_target_pairs={{0,64},{32,96},{64,0},{96,32},{128,192},{160,224},{192,128},{224,1... | collective-permute-start | bytes 405512 | tf_op jit(solution)/shard_map/ppermute | solution.py:212
  26.9 0.0 collective-permute-done.refs_0_
  26.9 0.2 collective-permute-start.5
  27.0 0.0 collective-permute-done.1.refs_1_
  27.1 2.6 %collective-permute-start.6 = (bf16[528,128]{1,0:T(8,128)(2,1)S(1)}, bf16[528,128]{1,0:T(8,128)(2,1)S(1)}, u32[]{:S(2)}, u32[]{:S(2)}) collective-permute-start(bf16[528,128]{1,0:T(8,128)(2,1)S(1)} %get-tuple-element.34), channel_id=1, source_target_pairs={{0,192},{32,224},{64,128},{96,160},{128,64},{160,96},{192,0},{224,... | collective-permute-start | bytes 405512 | tf_op jit(solution)/shard_map/ppermute | solution.py:212
  29.7 0.0 collective-permute-done.2.refs_2_
  29.7 0.0 collective-permute-done.3.refs_1_
  29.7 0.5 collective-permute-done.4.refs_2_
  30.2 4.6 %collective-permute-done.5.refs_3_ = bf16[528,128]{1,0:T(8,128)(2,1)S(1)} collective-permute-done((bf16[528,128]{1,0:T(8,128)(2,1)S(1)}, bf16[528,128]{1,0:T(8,128)(2,1)S(1)}, u32[]{:S(2)}, u32[]{:S(2)}) %collective-permute-start.5) | collective-permute-done | bytes 135200 | tf_op jit(solution)/shard_map/ppermute | solution.py:212
  34.8 0.0 collective-permute-done.6.refs_4_
  34.8 4.3 %all-to-all-done.kv_ref = bf16[256,2,256]{2,1,0:T(2,128)(2,1)S(1)} async-done(((bf16[256,2,256]{2,1,0:T(2,128)(2,1)}), bf16[256,2,256]{2,1,0:T(2,128)(2,1)S(1)}, u32[]{:S(2)}, u32[]{:S(2)}) %all-to-all-start) | async-done | bytes 262176 | tf_op jit(solution)/shard_map/all_to_all | solution.py:249
  39.1 4.5 %attention.1 = (bf16[512,128]{1,0:T(8,128)(2,1)S(1)}, bf16[512,128]{1,0:T(8,128)(2,1)S(1)}, bf16[512,128]{1,0:T(8,128)(2,1)S(1)}, bf16[512,128]{1,0:T(8,128)(2,1...) custom-call(f32[1]{0:T(128)} %bitcast.gate_ref, ...), custom_call_target="tpu_custom_call" | custom-call | tf_op jit(solution)/shard_map/attention/pallas_call | solution.py:200
  43.6 1.0 %collective-permute-start.10 = (bf16[512,128]{1,0:T(8,128)(2,1)S(1)}, bf16[512,128]{1,0:T(8,128)(2,1)S(1)}, u32[]{:S(2)}, u32[]{:S(2)}) collective-permute-start(bf16[512,128]{1,0:T(8,128)(2,1)S(1)} %get-tuple-element.39), channel_id=1, source_target_pairs={{0,128},{32,160},{64,192},{96,224},{128,0},{160,32},{192,64},{224,... | collective-permute-start | bytes 393224 | tf_op jit(solution)/shard_map/ppermute | solution.py:212
  44.6 1.4 %collective-permute-start.11 = (bf16[512,128]{1,0:T(8,128)(2,1)S(1)}, bf16[512,128]{1,0:T(8,128)(2,1)S(1)}, u32[]{:S(2)}, u32[]{:S(2)}) collective-permute-start(bf16[512,128]{1,0:T(8,128)(2,1)S(1)} %get-tuple-element.40), channel_id=1, source_target_pairs={{0,160},{32,128},{64,224},{96,192},{128,32},{160,0},{192,96},{224,... | collective-permute-start | bytes 393224 | tf_op jit(solution)/shard_map/ppermute | solution.py:212
  46.0 2.3 %collective-permute-start.12 = (bf16[512,128]{1,0:T(8,128)(2,1)S(1)}, bf16[512,128]{1,0:T(8,128)(2,1)S(1)}, u32[]{:S(2)}, u32[]{:S(2)}) collective-permute-start(bf16[512,128]{1,0:T(8,128)(2,1)S(1)} %get-tuple-element.41), channel_id=1, source_target_pairs={{0,224},{32,192},{64,160},{96,128},{128,96},{160,64},{192,32},{224... | collective-permute-start | bytes 393224 | tf_op jit(solution)/shard_map/ppermute | solution.py:212
  48.3 8.8 %all-to-all-start.1 = ((bf16[256,2,256]{2,1,0:T(2,128)(2,1)}), bf16[256,2,256]{2,1,0:T(2,128)(2,1)S(1)}, u32[]{:S(2)}, u32[]{:S(2)}) async-start(bf16[256,2,256]{2,1,0:T(2,128)(2,1)} %get-tuple-element.45), calls=%async_computation.1 | async-start | bytes 524288 | tf_op jit(solution)/shard_map/all_to_all | solution.py:272
  57.2 1.5 %collective-permute-start.7 = (bf16[512,128]{1,0:T(8,128)(2,1)S(1)}, bf16[512,128]{1,0:T(8,128)(2,1)S(1)}, u32[]{:S(2)}, u32[]{:S(2)}) collective-permute-start(bf16[512,128]{1,0:T(8,128)(2,1)S(1)} %get-tuple-element.36), channel_id=1, source_target_pairs={{0,32},{32,0},{64,96},{96,64},{128,160},{160,128},{192,224},{224,1... | collective-permute-start | bytes 393224 | tf_op jit(solution)/shard_map/ppermute | solution.py:212
  58.6 1.2 %collective-permute-start.8 = (bf16[512,128]{1,0:T(8,128)(2,1)S(1)}, bf16[512,128]{1,0:T(8,128)(2,1)S(1)}, u32[]{:S(2)}, u32[]{:S(2)}) collective-permute-start(bf16[512,128]{1,0:T(8,128)(2,1)S(1)} %get-tuple-element.37), channel_id=1, source_target_pairs={{0,64},{32,96},{64,0},{96,32},{128,192},{160,224},{192,128},{224,1... | collective-permute-start | bytes 393224 | tf_op jit(solution)/shard_map/ppermute | solution.py:212
  59.8 0.0 collective-permute-done.10.refs_0_
  59.8 0.1 collective-permute-start.9
  59.9 0.0 collective-permute-done.11.refs_1_
  59.9 2.6 %collective-permute-start.13 = (bf16[512,128]{1,0:T(8,128)(2,1)S(1)}, bf16[512,128]{1,0:T(8,128)(2,1)S(1)}, u32[]{:S(2)}, u32[]{:S(2)}) collective-permute-start(bf16[512,128]{1,0:T(8,128)(2,1)S(1)} %get-tuple-element.42), channel_id=1, source_target_pairs={{0,192},{32,224},{64,128},{96,160},{128,64},{160,96},{192,0},{224,... | collective-permute-start | bytes 393224 | tf_op jit(solution)/shard_map/ppermute | solution.py:212
  62.6 0.0 collective-permute-done.12.refs_2_
  62.6 0.0 collective-permute-done.7.refs_1_
  62.6 1.7 %collective-permute-done.8.refs_2_ = bf16[512,128]{1,0:T(8,128)(2,1)S(1)} collective-permute-done((bf16[512,128]{1,0:T(8,128)(2,1)S(1)}, bf16[512,128]{1,0:T(8,128)(2,1)S(1)}, u32[]{:S(2)}, u32[]{:S(2)}) %collective-permute-start.8) | collective-permute-done | bytes 131104 | tf_op jit(solution)/shard_map/ppermute | solution.py:212
  64.3 3.9 %collective-permute-done.9.refs_3_ = bf16[512,128]{1,0:T(8,128)(2,1)S(1)} collective-permute-done((bf16[512,128]{1,0:T(8,128)(2,1)S(1)}, bf16[512,128]{1,0:T(8,128)(2,1)S(1)}, u32[]{:S(2)}, u32[]{:S(2)}) %collective-permute-start.9) | collective-permute-done | bytes 131104 | tf_op jit(solution)/shard_map/ppermute | solution.py:212
  68.2 0.0 collective-permute-done.13.refs_6_
  68.2 1.1 %unpack.1 = (bf16[256,1024]{1,0:T(8,128)(2,1)}, bf16[256,1024]{1,0:T(8,128)(2,1)}) custom-call(bf16[512,128]{1,0:T(8,128)(2,1)S(1)} %get-tuple-element.35.refs_0_, bf16[512,128]{1,0:T(8,128)(2,1)S(1)} %collective-permute-done.7.refs_1_, bf16[512,128]{1,0:T(8,128)(2,1)S(1)} %collective-permute-done.8.refs_2_, ...), custom_call_target="tpu_custom_call" | custom-call | tf_op jit(solution)/shard_map/unpack/pallas_call | solution.py:200
  69.3 3.4 %all-to-all-done.1.in_ref = bf16[256,2,256]{2,1,0:T(2,128)(2,1)S(1)} async-done(((bf16[256,2,256]{2,1,0:T(2,128)(2,1)}), bf16[256,2,256]{2,1,0:T(2,128)(2,1)S(1)}, u32[]{:S(2)}, u32[]{:S(2)}) %all-to-all-start.1) | async-done | bytes 262176 | tf_op jit(solution)/shard_map/all_to_all | solution.py:272
  72.7 0.7 settle.1
  (3 shorter events, 0.1 us)
Async XLA Ops:
  2.9 24.0 %collective-permute-start = (bf16[528,128]{1,0:T(8,128)(2,1)S(1)}, bf16[528,128]{1,0:T(8,128)(2,1)S(1)}, u32[]{:S(2)}, u32[]{:S(2)}) collective-permute-start(bf16[528,128]{1,0:T(8,128)(2,1)S(1)} %get-tuple-element.27), channel_id=1, source_target_pairs={{0,128},{32,160},{64,192},{96,224},{128,0},{160,32},{192,64},{224,... | collective-permute-start | bytes 405512 | tf_op jit(solution)/shard_map/ppermute | solution.py:212
  6.7 20.3 %collective-permute-start.1 = (bf16[528,128]{1,0:T(8,128)(2,1)S(1)}, bf16[528,128]{1,0:T(8,128)(2,1)S(1)}, u32[]{:S(2)}, u32[]{:S(2)}) collective-permute-start(bf16[528,128]{1,0:T(8,128)(2,1)S(1)} %get-tuple-element.28), channel_id=1, source_target_pairs={{0,160},{32,128},{64,224},{96,192},{128,32},{160,0},{192,96},{224,... | collective-permute-start | bytes 405512 | tf_op jit(solution)/shard_map/ppermute | solution.py:212
  7.7 22.0 %collective-permute-start.2 = (bf16[528,128]{1,0:T(8,128)(2,1)S(1)}, bf16[528,128]{1,0:T(8,128)(2,1)S(1)}, u32[]{:S(2)}, u32[]{:S(2)}) collective-permute-start(bf16[528,128]{1,0:T(8,128)(2,1)S(1)} %get-tuple-element.29), channel_id=1, source_target_pairs={{0,224},{32,192},{64,160},{96,128},{128,96},{160,64},{192,32},{224... | collective-permute-start | bytes 405512 | tf_op jit(solution)/shard_map/ppermute | solution.py:212
  10.4 28.7 %all-to-all-start = ((bf16[256,2,256]{2,1,0:T(2,128)(2,1)}), bf16[256,2,256]{2,1,0:T(2,128)(2,1)S(1)}, u32[]{:S(2)}, u32[]{:S(2)}) async-start(bf16[256,2,256]{2,1,0:T(2,128)(2,1)} %get-tuple-element.26), calls=%async_computation | async-start | bytes 524288 | tf_op jit(solution)/shard_map/all_to_all | solution.py:249
  23.5 6.2 %collective-permute-start.3 = (bf16[528,128]{1,0:T(8,128)(2,1)S(1)}, bf16[528,128]{1,0:T(8,128)(2,1)S(1)}, u32[]{:S(2)}, u32[]{:S(2)}) collective-permute-start(bf16[528,128]{1,0:T(8,128)(2,1)S(1)} %get-tuple-element.31), channel_id=1, source_target_pairs={{0,32},{32,0},{64,96},{96,64},{128,160},{160,128},{192,224},{224,1... | collective-permute-start | bytes 405512 | tf_op jit(solution)/shard_map/ppermute | solution.py:212
  25.0 5.2 %collective-permute-start.4 = (bf16[528,128]{1,0:T(8,128)(2,1)S(1)}, bf16[528,128]{1,0:T(8,128)(2,1)S(1)}, u32[]{:S(2)}, u32[]{:S(2)}) collective-permute-start(bf16[528,128]{1,0:T(8,128)(2,1)S(1)} %get-tuple-element.32), channel_id=1, source_target_pairs={{0,64},{32,96},{64,0},{96,32},{128,192},{160,224},{192,128},{224,1... | collective-permute-start | bytes 405512 | tf_op jit(solution)/shard_map/ppermute | solution.py:212
  26.9 7.9 %collective-permute-start.5 = (bf16[528,128]{1,0:T(8,128)(2,1)S(1)}, bf16[528,128]{1,0:T(8,128)(2,1)S(1)}, u32[]{:S(2)}, u32[]{:S(2)}) collective-permute-start(bf16[528,128]{1,0:T(8,128)(2,1)S(1)} %get-tuple-element.33), channel_id=1, source_target_pairs={{0,96},{32,64},{64,32},{96,0},{128,224},{160,192},{192,160},{224,1... | collective-permute-start | bytes 405512 | tf_op jit(solution)/shard_map/ppermute | solution.py:212
  27.1 7.7 %collective-permute-start.6 = (bf16[528,128]{1,0:T(8,128)(2,1)S(1)}, bf16[528,128]{1,0:T(8,128)(2,1)S(1)}, u32[]{:S(2)}, u32[]{:S(2)}) collective-permute-start(bf16[528,128]{1,0:T(8,128)(2,1)S(1)} %get-tuple-element.34), channel_id=1, source_target_pairs={{0,192},{32,224},{64,128},{96,160},{128,64},{160,96},{192,0},{224,... | collective-permute-start | bytes 405512 | tf_op jit(solution)/shard_map/ppermute | solution.py:212
  43.6 16.2 %collective-permute-start.10 = (bf16[512,128]{1,0:T(8,128)(2,1)S(1)}, bf16[512,128]{1,0:T(8,128)(2,1)S(1)}, u32[]{:S(2)}, u32[]{:S(2)}) collective-permute-start(bf16[512,128]{1,0:T(8,128)(2,1)S(1)} %get-tuple-element.39), channel_id=1, source_target_pairs={{0,128},{32,160},{64,192},{96,224},{128,0},{160,32},{192,64},{224,... | collective-permute-start | bytes 393224 | tf_op jit(solution)/shard_map/ppermute | solution.py:212
  44.6 15.3 %collective-permute-start.11 = (bf16[512,128]{1,0:T(8,128)(2,1)S(1)}, bf16[512,128]{1,0:T(8,128)(2,1)S(1)}, u32[]{:S(2)}, u32[]{:S(2)}) collective-permute-start(bf16[512,128]{1,0:T(8,128)(2,1)S(1)} %get-tuple-element.40), channel_id=1, source_target_pairs={{0,160},{32,128},{64,224},{96,192},{128,32},{160,0},{192,96},{224,... | collective-permute-start | bytes 393224 | tf_op jit(solution)/shard_map/ppermute | solution.py:212
  46.0 16.5 %collective-permute-start.12 = (bf16[512,128]{1,0:T(8,128)(2,1)S(1)}, bf16[512,128]{1,0:T(8,128)(2,1)S(1)}, u32[]{:S(2)}, u32[]{:S(2)}) collective-permute-start(bf16[512,128]{1,0:T(8,128)(2,1)S(1)} %get-tuple-element.41), channel_id=1, source_target_pairs={{0,224},{32,192},{64,160},{96,128},{128,96},{160,64},{192,32},{224... | collective-permute-start | bytes 393224 | tf_op jit(solution)/shard_map/ppermute | solution.py:212
  48.3 24.4 %all-to-all-start.1 = ((bf16[256,2,256]{2,1,0:T(2,128)(2,1)}), bf16[256,2,256]{2,1,0:T(2,128)(2,1)S(1)}, u32[]{:S(2)}, u32[]{:S(2)}) async-start(bf16[256,2,256]{2,1,0:T(2,128)(2,1)} %get-tuple-element.45), calls=%async_computation.1 | async-start | bytes 524288 | tf_op jit(solution)/shard_map/all_to_all | solution.py:272
  57.2 5.5 %collective-permute-start.7 = (bf16[512,128]{1,0:T(8,128)(2,1)S(1)}, bf16[512,128]{1,0:T(8,128)(2,1)S(1)}, u32[]{:S(2)}, u32[]{:S(2)}) collective-permute-start(bf16[512,128]{1,0:T(8,128)(2,1)S(1)} %get-tuple-element.36), channel_id=1, source_target_pairs={{0,32},{32,0},{64,96},{96,64},{128,160},{160,128},{192,224},{224,1... | collective-permute-start | bytes 393224 | tf_op jit(solution)/shard_map/ppermute | solution.py:212
  58.6 5.7 %collective-permute-start.8 = (bf16[512,128]{1,0:T(8,128)(2,1)S(1)}, bf16[512,128]{1,0:T(8,128)(2,1)S(1)}, u32[]{:S(2)}, u32[]{:S(2)}) collective-permute-start(bf16[512,128]{1,0:T(8,128)(2,1)S(1)} %get-tuple-element.37), channel_id=1, source_target_pairs={{0,64},{32,96},{64,0},{96,32},{128,192},{160,224},{192,128},{224,1... | collective-permute-start | bytes 393224 | tf_op jit(solution)/shard_map/ppermute | solution.py:212
  59.8 8.4 %collective-permute-start.9 = (bf16[512,128]{1,0:T(8,128)(2,1)S(1)}, bf16[512,128]{1,0:T(8,128)(2,1)S(1)}, u32[]{:S(2)}, u32[]{:S(2)}) collective-permute-start(bf16[512,128]{1,0:T(8,128)(2,1)S(1)} %get-tuple-element.38), channel_id=1, source_target_pairs={{0,96},{32,64},{64,32},{96,0},{128,224},{160,192},{192,160},{224,1... | collective-permute-start | bytes 393224 | tf_op jit(solution)/shard_map/ppermute | solution.py:212
  59.9 8.3 %collective-permute-start.13 = (bf16[512,128]{1,0:T(8,128)(2,1)S(1)}, bf16[512,128]{1,0:T(8,128)(2,1)S(1)}, u32[]{:S(2)}, u32[]{:S(2)}) collective-permute-start(bf16[512,128]{1,0:T(8,128)(2,1)S(1)} %get-tuple-element.42), channel_id=1, source_target_pairs={{0,192},{32,224},{64,128},{96,160},{128,64},{160,96},{192,0},{224,... | collective-permute-start | bytes 393224 | tf_op jit(solution)/shard_map/ppermute | solution.py:212

commit v6 on v5

--- a/solution.py
+++ b/solution.py
@@ -10,7 +10,7 @@
 
 DH = 128
 TBLK = 128
-BLOCKS = 2
+BLOCKS = 4
 GROUP = 8
 HALVES = 1
 ZSIZE = 8

time: 73.7 us -> 73.7 us (level)
  no operation moved by 1% of the time
where the time goes in v6:
time: 73.7 us; the launch traced here: 73.5 us
  starting transfers between devices  45 us (61%)
  waiting for transfers between devices  18.3 us (25%)
  Pallas kernels  8.65 us (12%)
  between operations  1.41 us (2%)
    ppermute x14, starting transfers between devices, swap(): lax.ppermute(x, axis, [(i, i ^ k) for i in range(size)])  23.1 us
    all_to_all x1, starting transfers between devices, per_device(): both = lax.all_to_all(both, ORDER, 0, 0)  13.1 us
    ppermute x14, waiting for transfers between devices, swap(): lax.ppermute(x, axis, [(i, i ^ k) for i in range(size)])  10.6 us
    all_to_all x1, starting transfers between devices, per_device(): terms = lax.all_to_all(terms, ORDER, 0, 0)  8.86 us
    pallas_call x6, Pallas kernels, call(): pl.pallas_call(kernel, out_shape=shapes, in_specs=specs, out_specs=out_sp...  8.65 us
    all_to_all x1, waiting for transfers between devices, per_device(): both = lax.all_to_all(both, ORDER, 0, 0)  4.28 us
    all_to_all x1, waiting for transfers between devices, per_device(): terms = lax.all_to_all(terms, ORDER, 0, 0)  3.44 us
  transfers between devices with their start and end apart: 16, of which 6 were waited for; matrix products, arithmetic and copies ran while one was open for 0% of the time, Pallas kernels for 2%

profile of v6, /device:TPU:1, one launch (start us, length us, event | category | flops | bytes accessed | tf_op | source)
XLA Modules:
  0.0 73.5 jit_solution(17798318903022183423)
XLA Ops:
  0.6 2.2 %prepare.1 = (bf16[256,2,256]{2,1,0:T(2,128)(2,1)}, bf16[528,128]{1,0:T(8,128)(2,1)S(1)}, bf16[528,128]{1,0:T(8,128)(2,1)S(1)}, bf16[528,128]{1,0:T(8,128)(2,1)S...) custom-call(s32[2]{0:T(128)} %last_ref.1, ...), custom_call_target="tpu_custom_call" | custom-call | tf_op jit(solution)/shard_map/prepare/pallas_call | solution.py:200
  2.9 3.8 %collective-permute-start = (bf16[528,128]{1,0:T(8,128)(2,1)S(1)}, bf16[528,128]{1,0:T(8,128)(2,1)S(1)}, u32[]{:S(2)}, u32[]{:S(2)}) collective-permute-start(bf16[528,128]{1,0:T(8,128)(2,1)S(1)} %get-tuple-element.27), channel_id=1, source_target_pairs={{0,128},{32,160},{64,192},{96,224},{128,0},{160,32},{192,64},{224,... | collective-permute-start | bytes 405512 | tf_op jit(solution)/shard_map/ppermute | solution.py:212
  6.7 1.0 %collective-permute-start.1 = (bf16[528,128]{1,0:T(8,128)(2,1)S(1)}, bf16[528,128]{1,0:T(8,128)(2,1)S(1)}, u32[]{:S(2)}, u32[]{:S(2)}) collective-permute-start(bf16[528,128]{1,0:T(8,128)(2,1)S(1)} %get-tuple-element.28), channel_id=1, source_target_pairs={{0,160},{32,128},{64,224},{96,192},{128,32},{160,0},{192,96},{224,... | collective-permute-start | bytes 405512 | tf_op jit(solution)/shard_map/ppermute | solution.py:212
  7.7 2.7 %collective-permute-start.2 = (bf16[528,128]{1,0:T(8,128)(2,1)S(1)}, bf16[528,128]{1,0:T(8,128)(2,1)S(1)}, u32[]{:S(2)}, u32[]{:S(2)}) collective-permute-start(bf16[528,128]{1,0:T(8,128)(2,1)S(1)} %get-tuple-element.29), channel_id=1, source_target_pairs={{0,224},{32,192},{64,160},{96,128},{128,96},{160,64},{192,32},{224... | collective-permute-start | bytes 405512 | tf_op jit(solution)/shard_map/ppermute | solution.py:212
  10.4 13.1 %all-to-all-start = ((bf16[256,2,256]{2,1,0:T(2,128)(2,1)}), bf16[256,2,256]{2,1,0:T(2,128)(2,1)S(1)}, u32[]{:S(2)}, u32[]{:S(2)}) async-start(bf16[256,2,256]{2,1,0:T(2,128)(2,1)} %get-tuple-element.26), calls=%async_computation | async-start | bytes 524288 | tf_op jit(solution)/shard_map/all_to_all | solution.py:249
  23.5 1.5 %collective-permute-start.3 = (bf16[528,128]{1,0:T(8,128)(2,1)S(1)}, bf16[528,128]{1,0:T(8,128)(2,1)S(1)}, u32[]{:S(2)}, u32[]{:S(2)}) collective-permute-start(bf16[528,128]{1,0:T(8,128)(2,1)S(1)} %get-tuple-element.31), channel_id=1, source_target_pairs={{0,32},{32,0},{64,96},{96,64},{128,160},{160,128},{192,224},{224,1... | collective-permute-start | bytes 405512 | tf_op jit(solution)/shard_map/ppermute | solution.py:212
  25.0 1.2 %collective-permute-start.4 = (bf16[528,128]{1,0:T(8,128)(2,1)S(1)}, bf16[528,128]{1,0:T(8,128)(2,1)S(1)}, u32[]{:S(2)}, u32[]{:S(2)}) collective-permute-start(bf16[528,128]{1,0:T(8,128)(2,1)S(1)} %get-tuple-element.32), channel_id=1, source_target_pairs={{0,64},{32,96},{64,0},{96,32},{128,192},{160,224},{192,128},{224,1... | collective-permute-start | bytes 405512 | tf_op jit(solution)/shard_map/ppermute | solution.py:212
  26.9 0.0 collective-permute-done.refs_0_
  26.9 0.2 collective-permute-start.5
  27.0 0.0 collective-permute-done.1.refs_1_
  27.1 2.6 %collective-permute-start.6 = (bf16[528,128]{1,0:T(8,128)(2,1)S(1)}, bf16[528,128]{1,0:T(8,128)(2,1)S(1)}, u32[]{:S(2)}, u32[]{:S(2)}) collective-permute-start(bf16[528,128]{1,0:T(8,128)(2,1)S(1)} %get-tuple-element.34), channel_id=1, source_target_pairs={{0,192},{32,224},{64,128},{96,160},{128,64},{160,96},{192,0},{224,... | collective-permute-start | bytes 405512 | tf_op jit(solution)/shard_map/ppermute | solution.py:212
  29.7 0.0 collective-permute-done.2.refs_2_
  29.7 0.0 collective-permute-done.3.refs_1_
  29.7 0.5 collective-permute-done.4.refs_2_
  30.2 4.6 %collective-permute-done.5.refs_3_ = bf16[528,128]{1,0:T(8,128)(2,1)S(1)} collective-permute-done((bf16[528,128]{1,0:T(8,128)(2,1)S(1)}, bf16[528,128]{1,0:T(8,128)(2,1)S(1)}, u32[]{:S(2)}, u32[]{:S(2)}) %collective-permute-start.5) | collective-permute-done | bytes 135200 | tf_op jit(solution)/shard_map/ppermute | solution.py:212
  34.8 0.0 collective-permute-done.6.refs_4_
  34.8 4.3 %all-to-all-done.kv_ref = bf16[256,2,256]{2,1,0:T(2,128)(2,1)S(1)} async-done(((bf16[256,2,256]{2,1,0:T(2,128)(2,1)}), bf16[256,2,256]{2,1,0:T(2,128)(2,1)S(1)}, u32[]{:S(2)}, u32[]{:S(2)}) %all-to-all-start) | async-done | bytes 262176 | tf_op jit(solution)/shard_map/all_to_all | solution.py:249
  39.1 4.6 %attention.1 = (bf16[512,128]{1,0:T(8,128)(2,1)S(1)}, bf16[512,128]{1,0:T(8,128)(2,1)S(1)}, bf16[512,128]{1,0:T(8,128)(2,1)S(1)}, bf16[512,128]{1,0:T(8,128)(2,1...) custom-call(f32[1]{0:T(128)} %bitcast.gate_ref, ...), custom_call_target="tpu_custom_call" | custom-call | tf_op jit(solution)/shard_map/attention/pallas_call | solution.py:200
  43.6 1.0 %collective-permute-start.10 = (bf16[512,128]{1,0:T(8,128)(2,1)S(1)}, bf16[512,128]{1,0:T(8,128)(2,1)S(1)}, u32[]{:S(2)}, u32[]{:S(2)}) collective-permute-start(bf16[512,128]{1,0:T(8,128)(2,1)S(1)} %get-tuple-element.39), channel_id=1, source_target_pairs={{0,128},{32,160},{64,192},{96,224},{128,0},{160,32},{192,64},{224,... | collective-permute-start | bytes 393224 | tf_op jit(solution)/shard_map/ppermute | solution.py:212
  44.6 1.4 %collective-permute-start.11 = (bf16[512,128]{1,0:T(8,128)(2,1)S(1)}, bf16[512,128]{1,0:T(8,128)(2,1)S(1)}, u32[]{:S(2)}, u32[]{:S(2)}) collective-permute-start(bf16[512,128]{1,0:T(8,128)(2,1)S(1)} %get-tuple-element.40), channel_id=1, source_target_pairs={{0,160},{32,128},{64,224},{96,192},{128,32},{160,0},{192,96},{224,... | collective-permute-start | bytes 393224 | tf_op jit(solution)/shard_map/ppermute | solution.py:212
  46.1 2.3 %collective-permute-start.12 = (bf16[512,128]{1,0:T(8,128)(2,1)S(1)}, bf16[512,128]{1,0:T(8,128)(2,1)S(1)}, u32[]{:S(2)}, u32[]{:S(2)}) collective-permute-start(bf16[512,128]{1,0:T(8,128)(2,1)S(1)} %get-tuple-element.41), channel_id=1, source_target_pairs={{0,224},{32,192},{64,160},{96,128},{128,96},{160,64},{192,32},{224... | collective-permute-start | bytes 393224 | tf_op jit(solution)/shard_map/ppermute | solution.py:212
  48.3 8.9 %all-to-all-start.1 = ((bf16[256,2,256]{2,1,0:T(2,128)(2,1)}), bf16[256,2,256]{2,1,0:T(2,128)(2,1)S(1)}, u32[]{:S(2)}, u32[]{:S(2)}) async-start(bf16[256,2,256]{2,1,0:T(2,128)(2,1)} %get-tuple-element.45), calls=%async_computation.1 | async-start | bytes 524288 | tf_op jit(solution)/shard_map/all_to_all | solution.py:272
  57.2 1.5 %collective-permute-start.7 = (bf16[512,128]{1,0:T(8,128)(2,1)S(1)}, bf16[512,128]{1,0:T(8,128)(2,1)S(1)}, u32[]{:S(2)}, u32[]{:S(2)}) collective-permute-start(bf16[512,128]{1,0:T(8,128)(2,1)S(1)} %get-tuple-element.36), channel_id=1, source_target_pairs={{0,32},{32,0},{64,96},{96,64},{128,160},{160,128},{192,224},{224,1... | collective-permute-start | bytes 393224 | tf_op jit(solution)/shard_map/ppermute | solution.py:212
  58.7 1.2 %collective-permute-start.8 = (bf16[512,128]{1,0:T(8,128)(2,1)S(1)}, bf16[512,128]{1,0:T(8,128)(2,1)S(1)}, u32[]{:S(2)}, u32[]{:S(2)}) collective-permute-start(bf16[512,128]{1,0:T(8,128)(2,1)S(1)} %get-tuple-element.37), channel_id=1, source_target_pairs={{0,64},{32,96},{64,0},{96,32},{128,192},{160,224},{192,128},{224,1... | collective-permute-start | bytes 393224 | tf_op jit(solution)/shard_map/ppermute | solution.py:212
  59.9 0.0 collective-permute-done.10.refs_0_
  59.9 0.1 collective-permute-start.9
  60.0 0.0 collective-permute-done.11.refs_1_
  60.0 2.6 %collective-permute-start.13 = (bf16[512,128]{1,0:T(8,128)(2,1)S(1)}, bf16[512,128]{1,0:T(8,128)(2,1)S(1)}, u32[]{:S(2)}, u32[]{:S(2)}) collective-permute-start(bf16[512,128]{1,0:T(8,128)(2,1)S(1)} %get-tuple-element.42), channel_id=1, source_target_pairs={{0,192},{32,224},{64,128},{96,160},{128,64},{160,96},{192,0},{224,... | collective-permute-start | bytes 393224 | tf_op jit(solution)/shard_map/ppermute | solution.py:212
  62.6 0.0 collective-permute-done.12.refs_2_
  62.7 0.0 collective-permute-done.7.refs_1_
  62.7 1.7 %collective-permute-done.8.refs_2_ = bf16[512,128]{1,0:T(8,128)(2,1)S(1)} collective-permute-done((bf16[512,128]{1,0:T(8,128)(2,1)S(1)}, bf16[512,128]{1,0:T(8,128)(2,1)S(1)}, u32[]{:S(2)}, u32[]{:S(2)}) %collective-permute-start.8) | collective-permute-done | bytes 131104 | tf_op jit(solution)/shard_map/ppermute | solution.py:212
  64.4 3.9 %collective-permute-done.9.refs_3_ = bf16[512,128]{1,0:T(8,128)(2,1)S(1)} collective-permute-done((bf16[512,128]{1,0:T(8,128)(2,1)S(1)}, bf16[512,128]{1,0:T(8,128)(2,1)S(1)}, u32[]{:S(2)}, u32[]{:S(2)}) %collective-permute-start.9) | collective-permute-done | bytes 131104 | tf_op jit(solution)/shard_map/ppermute | solution.py:212
  68.2 0.0 collective-permute-done.13.refs_6_
  68.2 1.1 %unpack.1 = (bf16[256,1024]{1,0:T(8,128)(2,1)}, bf16[256,1024]{1,0:T(8,128)(2,1)}) custom-call(bf16[512,128]{1,0:T(8,128)(2,1)S(1)} %get-tuple-element.35.refs_0_, bf16[512,128]{1,0:T(8,128)(2,1)S(1)} %collective-permute-done.7.refs_1_, bf16[512,128]{1,0:T(8,128)(2,1)S(1)} %collective-permute-done.8.refs_2_, ...), custom_call_target="tpu_custom_call" | custom-call | tf_op jit(solution)/shard_map/unpack/pallas_call | solution.py:200
  69.3 3.4 %all-to-all-done.1.in_ref = bf16[256,2,256]{2,1,0:T(2,128)(2,1)S(1)} async-done(((bf16[256,2,256]{2,1,0:T(2,128)(2,1)}), bf16[256,2,256]{2,1,0:T(2,128)(2,1)S(1)}, u32[]{:S(2)}, u32[]{:S(2)}) %all-to-all-start.1) | async-done | bytes 262176 | tf_op jit(solution)/shard_map/all_to_all | solution.py:272
  72.8 0.7 settle.1
  (3 shorter events, 0.1 us)
Async XLA Ops:
  2.9 24.0 %collective-permute-start = (bf16[528,128]{1,0:T(8,128)(2,1)S(1)}, bf16[528,128]{1,0:T(8,128)(2,1)S(1)}, u32[]{:S(2)}, u32[]{:S(2)}) collective-permute-start(bf16[528,128]{1,0:T(8,128)(2,1)S(1)} %get-tuple-element.27), channel_id=1, source_target_pairs={{0,128},{32,160},{64,192},{96,224},{128,0},{160,32},{192,64},{224,... | collective-permute-start | bytes 405512 | tf_op jit(solution)/shard_map/ppermute | solution.py:212
  6.7 20.3 %collective-permute-start.1 = (bf16[528,128]{1,0:T(8,128)(2,1)S(1)}, bf16[528,128]{1,0:T(8,128)(2,1)S(1)}, u32[]{:S(2)}, u32[]{:S(2)}) collective-permute-start(bf16[528,128]{1,0:T(8,128)(2,1)S(1)} %get-tuple-element.28), channel_id=1, source_target_pairs={{0,160},{32,128},{64,224},{96,192},{128,32},{160,0},{192,96},{224,... | collective-permute-start | bytes 405512 | tf_op jit(solution)/shard_map/ppermute | solution.py:212
  7.7 22.0 %collective-permute-start.2 = (bf16[528,128]{1,0:T(8,128)(2,1)S(1)}, bf16[528,128]{1,0:T(8,128)(2,1)S(1)}, u32[]{:S(2)}, u32[]{:S(2)}) collective-permute-start(bf16[528,128]{1,0:T(8,128)(2,1)S(1)} %get-tuple-element.29), channel_id=1, source_target_pairs={{0,224},{32,192},{64,160},{96,128},{128,96},{160,64},{192,32},{224... | collective-permute-start | bytes 405512 | tf_op jit(solution)/shard_map/ppermute | solution.py:212
  10.4 28.7 %all-to-all-start = ((bf16[256,2,256]{2,1,0:T(2,128)(2,1)}), bf16[256,2,256]{2,1,0:T(2,128)(2,1)S(1)}, u32[]{:S(2)}, u32[]{:S(2)}) async-start(bf16[256,2,256]{2,1,0:T(2,128)(2,1)} %get-tuple-element.26), calls=%async_computation | async-start | bytes 524288 | tf_op jit(solution)/shard_map/all_to_all | solution.py:249
  23.5 6.2 %collective-permute-start.3 = (bf16[528,128]{1,0:T(8,128)(2,1)S(1)}, bf16[528,128]{1,0:T(8,128)(2,1)S(1)}, u32[]{:S(2)}, u32[]{:S(2)}) collective-permute-start(bf16[528,128]{1,0:T(8,128)(2,1)S(1)} %get-tuple-element.31), channel_id=1, source_target_pairs={{0,32},{32,0},{64,96},{96,64},{128,160},{160,128},{192,224},{224,1... | collective-permute-start | bytes 405512 | tf_op jit(solution)/shard_map/ppermute | solution.py:212
  25.0 5.2 %collective-permute-start.4 = (bf16[528,128]{1,0:T(8,128)(2,1)S(1)}, bf16[528,128]{1,0:T(8,128)(2,1)S(1)}, u32[]{:S(2)}, u32[]{:S(2)}) collective-permute-start(bf16[528,128]{1,0:T(8,128)(2,1)S(1)} %get-tuple-element.32), channel_id=1, source_target_pairs={{0,64},{32,96},{64,0},{96,32},{128,192},{160,224},{192,128},{224,1... | collective-permute-start | bytes 405512 | tf_op jit(solution)/shard_map/ppermute | solution.py:212
  26.9 7.9 %collective-permute-start.5 = (bf16[528,128]{1,0:T(8,128)(2,1)S(1)}, bf16[528,128]{1,0:T(8,128)(2,1)S(1)}, u32[]{:S(2)}, u32[]{:S(2)}) collective-permute-start(bf16[528,128]{1,0:T(8,128)(2,1)S(1)} %get-tuple-element.33), channel_id=1, source_target_pairs={{0,96},{32,64},{64,32},{96,0},{128,224},{160,192},{192,160},{224,1... | collective-permute-start | bytes 405512 | tf_op jit(solution)/shard_map/ppermute | solution.py:212
  27.1 7.7 %collective-permute-start.6 = (bf16[528,128]{1,0:T(8,128)(2,1)S(1)}, bf16[528,128]{1,0:T(8,128)(2,1)S(1)}, u32[]{:S(2)}, u32[]{:S(2)}) collective-permute-start(bf16[528,128]{1,0:T(8,128)(2,1)S(1)} %get-tuple-element.34), channel_id=1, source_target_pairs={{0,192},{32,224},{64,128},{96,160},{128,64},{160,96},{192,0},{224,... | collective-permute-start | bytes 405512 | tf_op jit(solution)/shard_map/ppermute | solution.py:212
  43.6 16.2 %collective-permute-start.10 = (bf16[512,128]{1,0:T(8,128)(2,1)S(1)}, bf16[512,128]{1,0:T(8,128)(2,1)S(1)}, u32[]{:S(2)}, u32[]{:S(2)}) collective-permute-start(bf16[512,128]{1,0:T(8,128)(2,1)S(1)} %get-tuple-element.39), channel_id=1, source_target_pairs={{0,128},{32,160},{64,192},{96,224},{128,0},{160,32},{192,64},{224,... | collective-permute-start | bytes 393224 | tf_op jit(solution)/shard_map/ppermute | solution.py:212
  44.6 15.3 %collective-permute-start.11 = (bf16[512,128]{1,0:T(8,128)(2,1)S(1)}, bf16[512,128]{1,0:T(8,128)(2,1)S(1)}, u32[]{:S(2)}, u32[]{:S(2)}) collective-permute-start(bf16[512,128]{1,0:T(8,128)(2,1)S(1)} %get-tuple-element.40), channel_id=1, source_target_pairs={{0,160},{32,128},{64,224},{96,192},{128,32},{160,0},{192,96},{224,... | collective-permute-start | bytes 393224 | tf_op jit(solution)/shard_map/ppermute | solution.py:212
  46.1 16.5 %collective-permute-start.12 = (bf16[512,128]{1,0:T(8,128)(2,1)S(1)}, bf16[512,128]{1,0:T(8,128)(2,1)S(1)}, u32[]{:S(2)}, u32[]{:S(2)}) collective-permute-start(bf16[512,128]{1,0:T(8,128)(2,1)S(1)} %get-tuple-element.41), channel_id=1, source_target_pairs={{0,224},{32,192},{64,160},{96,128},{128,96},{160,64},{192,32},{224... | collective-permute-start | bytes 393224 | tf_op jit(solution)/shard_map/ppermute | solution.py:212
  48.3 24.4 %all-to-all-start.1 = ((bf16[256,2,256]{2,1,0:T(2,128)(2,1)}), bf16[256,2,256]{2,1,0:T(2,128)(2,1)S(1)}, u32[]{:S(2)}, u32[]{:S(2)}) async-start(bf16[256,2,256]{2,1,0:T(2,128)(2,1)} %get-tuple-element.45), calls=%async_computation.1 | async-start | bytes 524288 | tf_op jit(solution)/shard_map/all_to_all | solution.py:272
  57.2 5.5 %collective-permute-start.7 = (bf16[512,128]{1,0:T(8,128)(2,1)S(1)}, bf16[512,128]{1,0:T(8,128)(2,1)S(1)}, u32[]{:S(2)}, u32[]{:S(2)}) collective-permute-start(bf16[512,128]{1,0:T(8,128)(2,1)S(1)} %get-tuple-element.36), channel_id=1, source_target_pairs={{0,32},{32,0},{64,96},{96,64},{128,160},{160,128},{192,224},{224,1... | collective-permute-start | bytes 393224 | tf_op jit(solution)/shard_map/ppermute | solution.py:212
  58.7 5.7 %collective-permute-start.8 = (bf16[512,128]{1,0:T(8,128)(2,1)S(1)}, bf16[512,128]{1,0:T(8,128)(2,1)S(1)}, u32[]{:S(2)}, u32[]{:S(2)}) collective-permute-start(bf16[512,128]{1,0:T(8,128)(2,1)S(1)} %get-tuple-element.37), channel_id=1, source_target_pairs={{0,64},{32,96},{64,0},{96,32},{128,192},{160,224},{192,128},{224,1... | collective-permute-start | bytes 393224 | tf_op jit(solution)/shard_map/ppermute | solution.py:212
  59.9 8.4 %collective-permute-start.9 = (bf16[512,128]{1,0:T(8,128)(2,1)S(1)}, bf16[512,128]{1,0:T(8,128)(2,1)S(1)}, u32[]{:S(2)}, u32[]{:S(2)}) collective-permute-start(bf16[512,128]{1,0:T(8,128)(2,1)S(1)} %get-tuple-element.38), channel_id=1, source_target_pairs={{0,96},{32,64},{64,32},{96,0},{128,224},{160,192},{192,160},{224,1... | collective-permute-start | bytes 393224 | tf_op jit(solution)/shard_map/ppermute | solution.py:212
  60.0 8.3 %collective-permute-start.13 = (bf16[512,128]{1,0:T(8,128)(2,1)S(1)}, bf16[512,128]{1,0:T(8,128)(2,1)S(1)}, u32[]{:S(2)}, u32[]{:S(2)}) collective-permute-start(bf16[512,128]{1,0:T(8,128)(2,1)S(1)} %get-tuple-element.42), channel_id=1, source_target_pairs={{0,192},{32,224},{64,128},{96,160},{128,64},{160,96},{192,0},{224,... | collective-permute-start | bytes 393224 | tf_op jit(solution)/shard_map/ppermute | solution.py:212
